TPU v7x, 256 devices: a whole 4x4x8 slice. The times are simulated.
256 devices in a mesh: tm: 16 (over x, y), space: 16 (over z, core).
Axes of the slice: x: 4, y: 4, z: 8, core: 2. Of those that a mesh axis runs over, the one named last changes fastest.
Arguments:
- snapshots: float32 [4096, 131072], P('tm', 'space'), may hold values from -300 to 300
- start: float32 [64, 2, 3, 32], replicated, may hold values from -6 to 6
Outputs:
- modes: float32 [64, 2, 3, 131072], P('tm', None, None, 'space')
- energies: float32 [64, 3], P('tm')
All inputs are finite; a program needn't handle non-finite values.
Results may differ from a plain program's by a relative error of at most 0.0003.
Values sent between devices are 32-bit elements; how exact they have to be, the bound alone decides.
No kernel may reach another device: no remote copies, remote signals or barrier semaphores. Data moves between devices by JAX's collectives and lax.ppermute only.
A program may use at most 128 MiB of HBM per device.

v0:
```python
import math

import jax
import jax.numpy as jnp
from jax import lax
from jax.sharding import PartitionSpec as P

NFFT = 128
FREQS = 64
NB = 32
ITERS = 2


EPSILON = 1e-06


def dft_table():
    time_ids = jnp.arange(NFFT, dtype=jnp.int32)
    freq_ids = jnp.arange(FREQS, dtype=jnp.int32)
    phase_ids = freq_ids[:, None] * time_ids[None, :] % NFFT
    angles = phase_ids.astype(jnp.float32) * (2.0 * math.pi / NFFT)
    window = 0.5 - 0.5 * jnp.cos(time_ids.astype(jnp.float32) * (2.0 * math.pi / NFFT))
    norm_scale = math.sqrt(8.0 / (3.0 * NFFT))
    cos_rows = jnp.cos(angles) * window[None, :] * norm_scale
    sin_rows = -jnp.sin(angles) * window[None, :] * norm_scale
    return jnp.stack([cos_rows, sin_rows], axis=1).reshape(2 * FREQS, NFFT)


def transform(block_data, basis_rows):
    block_count, _, point_count = block_data.shape
    product = jnp.einsum("kt,btx->kbx", basis_rows, block_data, precision=lax.Precision.HIGHEST)
    return product.reshape(FREQS, 2, block_count, point_count)


def partial_grams(spectra, total_points):
    freq_count, _, block_count, point_count = spectra.shape
    stacked = spectra.reshape(freq_count, 2 * block_count, point_count)
    products = jnp.einsum("fan,fcn->fac", stacked, stacked, precision=lax.Precision.HIGHEST) / (
        block_count * total_points
    )
    g_real = products[:, :block_count, :block_count] + products[:, block_count:, block_count:]
    g_imag = products[:, :block_count, block_count:] - products[:, block_count:, :block_count]
    return jnp.stack([g_real, g_imag], axis=1)


def batched(left, right):
    return jnp.einsum("fab,fmb->fma", left, right, precision=lax.Precision.HIGHEST)


def apply_gram(gram_parts, vectors):
    g_real, g_imag = (gram_parts[:, 0], gram_parts[:, 1])
    v_real, v_imag = (vectors[:, 0], vectors[:, 1])
    return jnp.stack(
        [
            batched(g_real, v_real) - batched(g_imag, v_imag),
            batched(g_real, v_imag) + batched(g_imag, v_real),
        ],
        axis=1,
    )


def orthonormal(vectors):
    columns = []
    for which in range(vectors.shape[2]):
        column = vectors[:, :, which, :]
        for earlier in columns:
            proj_real = jnp.sum(
                earlier[:, 0] * column[:, 0] + earlier[:, 1] * column[:, 1], axis=-1, keepdims=True
            )
            proj_imag = jnp.sum(
                earlier[:, 0] * column[:, 1] - earlier[:, 1] * column[:, 0], axis=-1, keepdims=True
            )
            column = column - jnp.stack(
                [
                    earlier[:, 0] * proj_real - earlier[:, 1] * proj_imag,
                    earlier[:, 0] * proj_imag + earlier[:, 1] * proj_real,
                ],
                axis=1,
            )
        col_norm = jnp.sqrt(jnp.sum(column * column, axis=(1, 2), keepdims=True) + EPSILON)
        columns.append(column / col_norm)
    return jnp.stack(columns, axis=2)


def leading(gram_parts, start):
    vectors = orthonormal(start)
    for sweep in range(ITERS):
        vectors = orthonormal(apply_gram(gram_parts, vectors))
    rayleigh = jnp.sum(vectors * apply_gram(gram_parts, vectors), axis=(1, 3))
    weights = vectors / jnp.sqrt(vectors.shape[3] * rayleigh)[:, None, :, None]
    return (rayleigh, weights)


def reconstruct(spectra, weights):
    freq_count, _, block_count, point_count = spectra.shape
    mode_count = weights.shape[2]
    w_real, w_imag = (weights[:, 0], weights[:, 1])
    coeffs = jnp.stack(
        [jnp.concatenate([w_real, -w_imag], axis=-1), jnp.concatenate([w_imag, w_real], axis=-1)],
        axis=1,
    )
    coeffs = coeffs.reshape(freq_count, 2 * mode_count, 2 * block_count)
    stacked = spectra.reshape(freq_count, 2 * block_count, point_count)
    result = jnp.einsum("fkc,fcn->fkn", coeffs, stacked, precision=lax.Precision.HIGHEST)
    return result.reshape(freq_count, 2, mode_count, point_count)


def on_device(snapshots, start):
    tm_count = lax.axis_size("tm")
    space_count = lax.axis_size("space")
    local_time, local_points = snapshots.shape
    total_points = local_points * space_count
    owned_freqs = FREQS // tm_count
    tm_index = lax.axis_index("tm")
    basis_rows = dft_table()
    regrouped = lax.all_to_all(snapshots, "tm", split_axis=1, concat_axis=0, tiled=True)
    spectra = transform(regrouped.reshape(NB, NFFT, regrouped.shape[1]), basis_rows)
    gram_parts = partial_grams(spectra, total_points)
    gram_whole = lax.psum(gram_parts, ("tm", "space"))
    rayleigh, weights = leading(gram_whole, start)
    energies = lax.dynamic_slice_in_dim(rayleigh, tm_index * owned_freqs, owned_freqs, 0)
    local_modes = reconstruct(spectra, weights)
    modes = lax.all_to_all(local_modes, "tm", split_axis=0, concat_axis=3, tiled=True)
    return (modes, energies)


def solution(mesh):
    in_specs = (P("tm", "space"), P())
    out_specs = (P("tm", None, None, "space"), P("tm", None))
    return jax.shard_map(
        on_device, mesh=mesh, in_specs=in_specs, out_specs=out_specs, check_vma=False
    )
```

profile of v0, /device:TPU:1, one launch (start us, length us, event | category | flops | bytes accessed | tf_op | source)
XLA Modules:
  0.0 524.0 jit_solution(6855811127937628939)
XLA Ops:
  7.2 8.0 %copy.272 = f32[32,16,8,512]{3,2,0,1:T(8,128)} copy(f32[32,16,8,512]{3,2,1,0:T(8,128)} %bitcast.178) | data formatting | bytes 16777216 | tf_op jit(solution)/shard_map/all_to_all | solution.py:116
  15.2 7.8 %all-to-all-start = ((f32[256,16,512]{2,0,1:T(8,128)}), f32[256,16,512]{2,0,1:T(8,128)}, u32[]{:S(2)}, u32[]{:S(2)}) async-start(f32[256,16,512]{2,0,1:T(8,128)} %bitcast.177), calls=%async_computation | async-start | bytes 16777216 | tf_op jit(solution)/shard_map/all_to_all | solution.py:116
  23.1 0.2 multiply_multiply_fusion.1
  23.6 145.5 %all-to-all-done = f32[256,16,512]{2,0,1:T(8,128)} async-done(((f32[256,16,512]{2,0,1:T(8,128)}), f32[256,16,512]{2,0,1:T(8,128)}, u32[]{:S(2)}, u32[]{:S(2)}) %all-to-all-start) | async-done | bytes 8388640 | tf_op jit(solution)/shard_map/all_to_all | solution.py:116
  169.1 12.0 %fusion.46 = f32[128,32,512]{2,0,1:T(8,128)S(1)} fusion(f32[128,128,1]{1,0,2:T(8,128)S(1)} %bitcast.187, f32[32,128,512]{2,1,0:T(8,128)} %bitcast.16), kind=kOutput, calls=%fused_computation.169 | convolution fusion | flops 3221225472 | bytes 16842752 | tf_op jit(solution)/shard_map/kt,btx->kbx/dot_general | solution.py:31
  181.1 4.9 copy.223
  186.0 8.2 %convolution_multiply_fusion = f32[64,64,64]{2,1,0:T(8,128)S(1)} fusion(f32[64,64,512]{2,1,0:T(8,128)S(1)} %bitcast.175), kind=kOutput, calls=%fused_computation.2 | convolution fusion | flops 1610874880 | bytes 9437184 | tf_op jit(solution)/shard_map/fan,fcn->fac/dot_general | solution.py:38
  194.2 0.6 fusion.1
  194.8 1.5 pad_maximum_fusion
  196.4 0.1 copy.225
  196.5 0.1 copy.224
  196.6 265.6 %all-reduce.2.cloned.1.call-done = f32[64,2,32,32]{3,2,0,1:T(8,128)} async-done(((f32[64,2,32,32]{3,2,0,1:T(8,128)}), f32[64,2,32,32]{3,2,0,1:T(8,128)}) %all-reduce.2.cloned.1.call-update) | async-done | bytes 524304 | tf_op jit(solution)/shard_map/psum | solution.py:119
  462.3 3.1 fusion.13
  465.4 0.1 copy.227
  465.5 3.0 fusion.7
  468.4 0.1 copy.226
  468.5 1.8 fusion.12
  470.3 0.1 copy.231
  470.4 1.8 fusion.6
  472.2 0.1 copy.230
  472.7 0.1 copy.236
  472.8 1.7 fusion.11
  474.5 0.1 copy.238
  474.6 0.1 copy.235
  474.8 1.7 fusion.5
  476.5 0.1 copy.237
  476.6 2.0 fusion.10
  478.6 0.1 copy.242
  478.7 1.8 fusion.4
  480.4 0.1 copy.241
  480.9 0.1 copy.247
  481.1 1.7 fusion.9
  482.8 0.1 copy.249
  482.9 0.1 copy.246
  483.0 1.7 fusion.3
  484.8 0.1 copy.248
  484.9 1.8 fusion.8
  486.6 0.1 copy.253
  486.7 1.8 fusion.2
  488.5 0.1 copy.252
  488.8 0.1 copy.255
  488.9 6.4 %fusion.47 = f32[64,6,512]{2,1,0:T(8,128)S(1)} fusion(f32[64,6,64]{2,1,0:T(8,128)S(1)} %copy.255, f32[64,64,512]{2,1,0:T(8,128)} %bitcast.176), kind=kOutput, calls=%fused_computation.170 | convolution fusion | flops 150994944 | bytes 9273344 | tf_op jit(solution)/shard_map/fkc,fcn->fkn/dot_general | solution.py:104
  495.4 0.5 copy.256
  495.8 1.5 copy.257
  497.3 6.4 %all-to-all-start.1 = ((f32[64,2,3,512]{3,1,2,0:T(2,128)}), f32[64,2,3,512]{3,1,2,0:T(2,128)S(1)}, u32[]{:S(2)}, u32[]{:S(2)}) async-start(f32[64,2,3,512]{3,1,2,0:T(2,128)} %copy.257), calls=%async_computation.1 | async-start | bytes 1572864 | tf_op jit(solution)/shard_map/all_to_all | solution.py:123
  503.8 0.7 copy.259
  504.5 11.3 %all-to-all-done.1 = f32[64,2,3,512]{3,1,2,0:T(2,128)S(1)} async-done(((f32[64,2,3,512]{3,1,2,0:T(2,128)}), f32[64,2,3,512]{3,1,2,0:T(2,128)S(1)}, u32[]{:S(2)}, u32[]{:S(2)}) %all-to-all-start.1) | async-done | bytes 786464 | tf_op jit(solution)/shard_map/all_to_all | solution.py:123
  515.7 1.3 copy.270
  (78 shorter events, 1.3 us)
Async XLA Ops:
  15.2 8.1 %copy-start.2 = (f32[64,2,3,32]{0,3,2,1:T(8,128)S(1)}, f32[64,2,3,32]{0,3,2,1:T(8,128)}, u32[]{:S(2)}) copy-start(f32[64,2,3,32]{0,3,2,1:T(8,128)} %param.3) | copy-start | bytes 147460
  15.2 153.9 %all-to-all-start = ((f32[256,16,512]{2,0,1:T(8,128)}), f32[256,16,512]{2,0,1:T(8,128)}, u32[]{:S(2)}, u32[]{:S(2)}) async-start(f32[256,16,512]{2,0,1:T(8,128)} %bitcast.177), calls=%async_computation | async-start | bytes 16777216 | tf_op jit(solution)/shard_map/all_to_all | solution.py:116
  23.0 439.3 %all-reduce.2.cloned.1.call-start = ((), (), s32[]{:S(2)}) async-start(), calls=%async_computation.2 | async-start | bytes 4194304 | tf_op jit(solution)/shard_map/psum | solution.py:119
  186.0 8.2 %copy-start = (f32[128,32,512]{2,1,0:T(8,128)}, f32[128,32,512]{2,1,0:T(8,128)S(1)}, u32[]{:S(2)}) copy-start(f32[128,32,512]{2,1,0:T(8,128)S(1)} %copy.223) | copy-start | bytes 25165828
  462.3 6.3 %copy-start.1 = (f32[64,2,32,32]{3,2,0,1:T(8,128)S(1)}, f32[64,2,32,32]{3,2,0,1:T(8,128)}, u32[]{:S(2)}) copy-start(f32[64,2,32,32]{3,2,0,1:T(8,128)} %all-reduce.2.cloned.1.call-done) | copy-start | bytes 1572868
  497.3 18.4 %all-to-all-start.1 = ((f32[64,2,3,512]{3,1,2,0:T(2,128)}), f32[64,2,3,512]{3,1,2,0:T(2,128)S(1)}, u32[]{:S(2)}, u32[]{:S(2)}) async-start(f32[64,2,3,512]{3,1,2,0:T(2,128)} %copy.257), calls=%async_computation.1 | async-start | bytes 1572864 | tf_op jit(solution)/shard_map/all_to_all | solution.py:123
Sparse Core Ops, SparseCore 0:
  196.5 265.7 all-reduce.1
where the time goes:
time: 531 us; the launch traced here: 524 us
  waiting for transfers between devices  422 us (79%)
  matrix products  50.5 us (10%)
  local copies, waits for them, and re-layouts  18.8 us (4%)
  between operations  14.8 us (3%)
  starting transfers between devices  14.2 us (3%)
    psum x1, waiting for transfers between devices, on_device(): gram_whole = lax.psum(gram_parts, ('tm', 'space'))  266 us
    all_to_all x1, waiting for transfers between devices, on_device(): lax.all_to_all(snapshots, 'tm', split_axis=1, concat_axis=0, tiled=True)  146 us
    dot_general x12, matrix products, batched(): jnp.einsum('fab,fmb->fma', left, right, precision=lax.Precision.HIGHEST)  23.9 us
    dot_general x1, matrix products, transform(): jnp.einsum('kt,btx->kbx', basis_rows, block_data, precision=lax.Precision...  12 us
    all_to_all x1, waiting for transfers between devices, on_device(): lax.all_to_all(local_modes, 'tm', split_axis=0, concat_axis=3, tiled=True)  11.3 us
  transfers between devices with their start and end apart: 3, of which 3 were waited for; matrix products, arithmetic and copies ran while one was open for 0% of the time, Pallas kernels for 0%

commit v1 on v0

v1 whole, which is shorter than its diff:
```python
import functools
import math

import jax
import jax.numpy as jnp
import numpy as np
from jax import lax
from jax.experimental import pallas as pl
from jax.experimental.pallas import tpu as pltpu
from jax.sharding import PartitionSpec as P

NFFT = 128
FREQS = 64
NB = 32
MODES = 3
ITERS = 2
EPSILON = 1e-06
F32 = jnp.float32
BF16 = jnp.bfloat16
EXACT = lax.Precision.HIGHEST
VMEM_LIMIT = 48 * 1024 * 1024


def dft_table():
    time_ids = np.arange(NFFT)
    phase = np.arange(FREQS)[:, None] * time_ids[None, :] % NFFT
    angles = phase * (2.0 * math.pi / NFFT)
    window = 0.5 - 0.5 * np.cos(time_ids * (2.0 * math.pi / NFFT))
    scaled = window[None, :] * math.sqrt(8.0 / (3.0 * NFFT))
    return np.stack([np.cos(angles) * scaled, -np.sin(angles) * scaled], axis=1)


def send_rows(owners, local_blocks):
    table = dft_table().reshape(owners, 1, -1, NFFT)
    rows = np.zeros((owners, local_blocks, table.shape[2], local_blocks, NFFT))
    for block in range(local_blocks):
        rows[:, block, :, block, :] = table[:, 0]
    rows = rows.reshape(-1, local_blocks * NFFT).astype(np.float32)
    high = rows.astype(BF16)
    low = (rows - high.astype(np.float32)).astype(BF16)
    return high, low


def split(value):
    high = value.astype(BF16)
    return high, (value - high.astype(F32)).astype(BF16)


def dot(left, right):
    return jnp.dot(left, right, preferred_element_type=F32)


def exact_dot(left, right):
    return jnp.dot(left, right, precision=EXACT, preferred_element_type=F32)


def iota(shape, dim):
    return lax.broadcasted_iota(jnp.int32, shape, dim)


def transform_kernel(high_ref, low_ref, x_ref, out_ref):
    x_high, x_low = split(x_ref[...])
    high = high_ref[...]
    out = dot(high, x_high) + (dot(high, x_low) + dot(low_ref[...], x_high))
    out_ref[...] = out.reshape(out_ref.shape)


def transform(snapshots, owners):
    times, points = snapshots.shape
    local_blocks = times // NFFT
    high, low = send_rows(owners, local_blocks)
    tile = min(2048, points)
    per_owner = high.shape[0] // owners
    whole = pl.BlockSpec(high.shape, lambda i: (0, 0))
    return pl.pallas_call(
        transform_kernel,
        grid=(points // tile,),
        in_specs=[whole, whole, pl.BlockSpec((times, tile), lambda i: (0, i))],
        out_specs=pl.BlockSpec((owners, per_owner, tile), lambda i: (0, 0, i)),
        out_shape=jax.ShapeDtypeStruct((owners, per_owner, points), F32),
        compiler_params=pltpu.CompilerParams(vmem_limit_bytes=VMEM_LIMIT),
        name="transform",
    )(jnp.asarray(high), jnp.asarray(low), snapshots)


def gram_kernel(bins, scale, copies, s_ref, out_ref, same_ref, cross_ref):
    step = pl.program_id(0)
    rows = s_ref.shape[0] * s_ref.shape[1]
    half = rows // 2

    @pl.when(step == 0)
    def _():
        same_ref[...] = jnp.zeros_like(same_ref)
        cross_ref[...] = jnp.zeros_like(cross_ref)

    high, low = split(s_ref[...].reshape(rows, s_ref.shape[2]))
    contract = (((1,), (1,)), ((), ()))
    same_ref[...] += lax.dot_general(high, high, contract, preferred_element_type=F32)
    cross_ref[...] += lax.dot_general(high, low, contract, preferred_element_type=F32)

    @pl.when(step == pl.num_programs(0) - 1)
    def _():
        cross = cross_ref[...]
        full = (same_ref[...] + (cross + cross.T)) * scale
        row, col = iota((rows, rows), 0), iota((rows, rows), 1)
        full = jnp.where((row >> 1) % bins == (col >> 1) % bins, full, 0.0)
        spread = jnp.where(col == (row & 1) * half + (row >> 1), 1.0, 0.0)
        row, col = iota((2 * NB, rows), 0), iota((2 * NB, rows), 1)
        fold = jnp.where(row == (col & 1) * NB + (col >> 1) // bins, 1.0, 0.0)
        part = exact_dot(exact_dot(fold, full), spread)
        real = part[:NB, :half] + part[NB:, half:]
        imag = part[NB:, :half] - part[:NB, half:]
        both = jnp.concatenate([real, imag], axis=1)
        for copy in range(copies):
            out_ref[copy] = both


def partial_gram(spectra, bins, total_points, copies):
    owners, per_owner, points = spectra.shape
    rows = owners * per_owner
    tile = min(2048, points)
    scale = 1.0 / (NB * total_points)
    return pl.pallas_call(
        functools.partial(gram_kernel, bins, scale, copies),
        grid=(points // tile,),
        in_specs=[pl.BlockSpec((owners, per_owner, tile), lambda i: (0, 0, i))],
        out_specs=pl.BlockSpec((copies, NB, rows), lambda i: (0, 0, 0)),
        out_shape=jax.ShapeDtypeStruct((copies, NB, rows), F32),
        scratch_shapes=[pltpu.VMEM((rows, rows), F32), pltpu.VMEM((rows, rows), F32)],
        compiler_params=pltpu.CompilerParams(vmem_limit_bytes=VMEM_LIMIT),
        name="gram",
    )(spectra)


def block_sum(value, bins):
    shift = bins
    while shift < value.shape[1]:
        value = value + pltpu.roll(value, shift, 1)
        shift *= 2
    return value


def orthonormal(real, imag, bins):
    done = []
    for which in range(MODES):
        c_real, c_imag = real[which : which + 1], imag[which : which + 1]
        for e_real, e_imag in done:
            proj_real = block_sum(e_real * c_real + e_imag * c_imag, bins)
            proj_imag = block_sum(e_real * c_imag - e_imag * c_real, bins)
            c_real, c_imag = (
                c_real - (e_real * proj_real - e_imag * proj_imag),
                c_imag - (e_real * proj_imag + e_imag * proj_real),
            )
        norm = jnp.sqrt(block_sum(c_real * c_real + c_imag * c_imag, bins) + EPSILON)
        done.append((c_real / norm, c_imag / norm))
    pad = [jnp.zeros((8 - MODES, real.shape[1]), F32)]
    return (
        jnp.concatenate([c[0] for c in done] + pad, axis=0),
        jnp.concatenate([c[1] for c in done] + pad, axis=0),
    )


def apply_gram(gram, real, imag):
    lanes = real.shape[1]
    product = exact_dot(jnp.concatenate([real, imag], axis=0), gram)
    return (
        product[:8, :lanes] - product[8:, lanes:],
        product[8:, :lanes] + product[:8, lanes:],
    )


def leading(gram_parts, start, bins):
    lanes = start.shape[1]
    total = gram_parts[0]
    for part in gram_parts[1:]:
        total = total + part
    row, col = iota((lanes, NB), 0), iota((lanes, NB), 1)
    spread = jnp.where(row // bins == col, 1.0, 0.0)
    gram = exact_dot(spread, total)
    row, col = iota(gram.shape, 0), iota(gram.shape, 1)
    gram = jnp.where(row % bins == col % bins, gram, 0.0)
    real, imag = orthonormal(start[:8], start[8:], bins)
    for _ in range(ITERS):
        real, imag = orthonormal(*apply_gram(gram, real, imag), bins)
    g_real, g_imag = apply_gram(gram, real, imag)
    rayleigh = block_sum(real * g_real + imag * g_imag, bins)
    norm = jnp.sqrt(NB * rayleigh)
    used = iota(real.shape, 0) < MODES
    return (
        jnp.where(used, real / norm, 0.0),
        jnp.where(used, imag / norm, 0.0),
        rayleigh,
    )


def modes_kernel(bins, gram_ref, start_ref, s_ref, modes_ref, energy_ref, coef_ref):
    rows = s_ref.shape[0] * s_ref.shape[1]
    half = rows // 2

    @pl.when(pl.program_id(0) == 0)
    def _():
        parts = [gram_ref[i] for i in range(gram_ref.shape[0])]
        real, imag, rayleigh = leading(parts, start_ref[...], bins)
        energy_ref[...] = rayleigh
        row, col = iota((half, rows), 0), iota((half, rows), 1)
        to_real = jnp.where(col == 2 * row, 1.0, 0.0)
        to_imag = jnp.where(col == 2 * row + 1, 1.0, 0.0)
        coefs = (
            exact_dot(real, to_real) - exact_dot(imag, to_imag),
            exact_dot(imag, to_real) + exact_dot(real, to_imag),
        )
        owner = (iota((8, rows), 1) >> 1) % bins
        stacked = jnp.concatenate(
            [jnp.where(owner == k, coefs[p], 0.0) for k in range(bins) for p in range(2)],
            axis=0,
        )
        high, low = split(stacked)
        coef_ref[0] = high
        coef_ref[1] = low

    s_high, s_low = split(s_ref[...].reshape(rows, s_ref.shape[2]))
    c_high, c_low = coef_ref[0], coef_ref[1]
    out = dot(c_high, s_high) + (dot(c_high, s_low) + dot(c_low, s_high))
    for k in range(bins):
        for p in range(2):
            at = (2 * k + p) * 8
            modes_ref[k, p] = out[at : at + MODES]


def modes_of(gram_parts, start, spectra, bins):
    owners, per_owner, points = spectra.shape
    rows = owners * per_owner
    tile = min(2048, points)
    lanes = start.shape[1]
    return pl.pallas_call(
        functools.partial(modes_kernel, bins),
        grid=(points // tile,),
        in_specs=[
            pl.BlockSpec(gram_parts.shape, lambda i: (0, 0, 0)),
            pl.BlockSpec(start.shape, lambda i: (0, 0)),
            pl.BlockSpec((owners, per_owner, tile), lambda i: (0, 0, i)),
        ],
        out_specs=[
            pl.BlockSpec((bins, 2, MODES, tile), lambda i: (0, 0, 0, i)),
            pl.BlockSpec((8, lanes), lambda i: (0, 0)),
        ],
        out_shape=[
            jax.ShapeDtypeStruct((bins, 2, MODES, points), F32),
            jax.ShapeDtypeStruct((8, lanes), F32),
        ],
        scratch_shapes=[pltpu.VMEM((2, 16 * bins, rows), BF16)],
        compiler_params=pltpu.CompilerParams(vmem_limit_bytes=VMEM_LIMIT),
        name="modes",
    )(gram_parts, start, spectra)


def on_device(snapshots, start):
    tm_count = lax.axis_size("tm")
    space_count = lax.axis_size("space")
    total_points = snapshots.shape[1] * space_count
    bins = FREQS // tm_count
    first = lax.axis_index("tm") * bins
    own = lax.dynamic_slice_in_dim(start, first, bins, 0)
    own = jnp.pad(own.transpose(1, 2, 3, 0), ((0, 0), (0, 8 - MODES), (0, 0), (0, 0)))
    own = own.reshape(16, NB * bins)
    sent = transform(snapshots, tm_count)
    spectra = lax.all_to_all(sent, "tm", split_axis=0, concat_axis=0, tiled=True)
    gram = partial_gram(spectra, bins, total_points, space_count)
    grams = lax.all_to_all(gram, "space", split_axis=0, concat_axis=0, tiled=True)
    modes, rayleigh = modes_of(grams, own, spectra, bins)
    return (modes, rayleigh[:MODES, :bins].T)


def solution(mesh):
    in_specs = (P("tm", "space"), P())
    out_specs = (P("tm", None, None, "space"), P("tm", None))
    return jax.shard_map(
        on_device, mesh=mesh, in_specs=in_specs, out_specs=out_specs, check_vma=False
    )
```

time: 531 us -> 164 us (0.31); the launches traced: 524 us -> 164 us
  waiting for transfers between devices: 422 us -> 17 us
  blocking collectives: 0 us -> 102 us
  matrix products: 50.5 us -> 0 us
  Pallas kernels: 0 us -> 28.5 us
  local copies, waits for them, and re-layouts: 18.8 us -> 4.27 us
  between operations: 14.8 us -> 0.68 us
    psum x1 -> x0, waiting for transfers between devices: 266 us -> none  [on_device(): gram_whole = lax.psum(gram_parts, ('tm', 'space'))]
    all_to_all x2 -> x1, waiting for transfers between devices: 157 us -> 17 us  [on_device(): lax.all_to_all(gram, 'space', split_axis=0, concat_axis=0, tiled=True)]
    all_to_all x0 -> x1, blocking collectives: none -> 102 us  [on_device(): lax.all_to_all(sent, 'tm', split_axis=0, concat_axis=0, tiled=True)]
    dot_general x15 -> x0, matrix products: 50.5 us -> none  [the longest x12 23.9 us: batched(): jnp.einsum('fab,fmb->fma', left, right, precision=lax.Precision.HIGHEST)]
    pallas_call x0 -> x3, Pallas kernels: none -> 28.5 us  [the longest x1 12.3 us: modes_of(): pl.pallas_call(functools.partial(modes_kernel, bins), grid=(points // til...]
    all_to_all x2 -> x0, local copies, waits for them, and re-layouts: 9.27 us -> none  [the longest x1 8.02 us: on_device(): lax.all_to_all(snapshots, 'tm', split_axis=1, concat_axis=0, tiled=True)]
    dot_general x14 -> x0, local copies, waits for them, and re-layouts: 6.36 us -> none  [the longest x1 4.86 us: transform(): jnp.einsum('kt,btx->kbx', basis_rows, block_data, precision=lax.Precision...]
    all_to_all x2 -> x1, starting transfers between devices: 14.2 us -> 11.1 us  [on_device(): lax.all_to_all(gram, 'space', split_axis=0, concat_axis=0, tiled=True)]
  transfers between devices with their start and end apart: 3 -> 1, of which waited for: 3 -> 1; matrix products, arithmetic and copies ran while one was open for 0% -> 0% of each run, Pallas kernels for 0% -> 0%
where the time goes in v1:
time: 164 us
  blocking collectives  102 us (62%)
  Pallas kernels  28.5 us (17%)
  waiting for transfers between devices  17 us (10%)
  starting transfers between devices  11.1 us (7%)
  local copies, waits for them, and re-layouts  4.27 us (3%)
    all_to_all x1, blocking collectives, on_device(): lax.all_to_all(sent, 'tm', split_axis=0, concat_axis=0, tiled=True)  102 us
    all_to_all x1, waiting for transfers between devices, on_device(): lax.all_to_all(gram, 'space', split_axis=0, concat_axis=0, tiled=True)  17 us
    pallas_call x1, Pallas kernels, modes_of(): pl.pallas_call(functools.partial(modes_kernel, bins), grid=(points // til...  12.3 us
    all_to_all x1, starting transfers between devices, on_device(): lax.all_to_all(gram, 'space', split_axis=0, concat_axis=0, tiled=True)  11.1 us
    pallas_call x1, Pallas kernels, transform(): pl.pallas_call(transform_kernel, grid=(points // tile,), in_specs=[whole,...  8.95 us
    pallas_call x1, Pallas kernels, partial_gram(): pl.pallas_call(functools.partial(gram_kernel, bins, scale, copies), grid=...  7.26 us
    unnamed x8, local copies, waits for them, and re-layouts  4 us
  transfers between devices with their start and end apart: 1, of which 1 were waited for; matrix products, arithmetic and copies ran while one was open for 0% of the time, Pallas kernels for 0%

profile of v1, /device:TPU:1, one launch (start us, length us, event | category | flops | bytes accessed | tf_op | source)
XLA Modules:
  0.0 163.9 jit_solution(18426551147552392)
XLA Ops:
  0.6 0.0 copy-start
  0.6 0.0 copy-start.1
  0.7 0.9 copy-done.1
  1.6 0.0 copy-start.2
  1.6 0.9 copy-done.2
  2.5 9.0 %transform.1 = f32[16,16,8192]{2,1,0:T(8,128)} custom-call(bf16[256,256]{1,0:T(8,128)(2,1)S(1)} %copy-done.1, bf16[256,256]{1,0:T(8,128)(2,1)S(1)} %copy-done.2, f32[256,8192]{1,0:T(8,128)} %x_ref.1), custom_call_target="tpu_custom_call" | custom-call | tf_op jit(solution)/shard_map/transform/pallas_call | solution.py:75
  11.4 102.4 %all_to_all.10.s_ref = f32[16,16,8192]{2,1,0:T(8,128)} all-to-all(f32[16,16,8192]{2,1,0:T(8,128)} %transform.1), channel_id=1, replica_groups=mesh['tm'=16,'space'=16] {'tm'}, dimensions={0} | all-to-all | bytes 16777216 | tf_op jit(solution)/shard_map/all_to_all | solution.py:267
  113.8 7.3 %gram.1 = f32[16,32,256]{2,1,0:T(8,128)} custom-call(f32[16,16,8192]{2,1,0:T(8,128)} %all_to_all.10.s_ref), custom_call_target="tpu_custom_call" | custom-call | tf_op jit(solution)/shard_map/gram/pallas_call | solution.py:123
  121.1 11.1 %all-to-all-start.1 = ((f32[16,32,256]{2,1,0:T(8,128)}), f32[16,32,256]{2,1,0:T(8,128)S(1)}, u32[]{:S(2)}, u32[]{:S(2)}) async-start(f32[16,32,256]{2,1,0:T(8,128)} %gram.1), calls=%async_computation.1 | async-start | bytes 1048576 | tf_op jit(solution)/shard_map/all_to_all | solution.py:269
  132.2 0.0 copy-done
  132.2 0.1 dynamic-slice_bitcast_fusion
  132.3 0.2 reshape.8.start_ref
  132.4 17.0 %all-to-all-done.1.gram_ref = f32[16,32,256]{2,1,0:T(8,128)S(1)} async-done(((f32[16,32,256]{2,1,0:T(8,128)}), f32[16,32,256]{2,1,0:T(8,128)S(1)}, u32[]{:S(2)}, u32[]{:S(2)}) %all-to-all-start.1) | async-done | bytes 524320 | tf_op jit(solution)/shard_map/all_to_all | solution.py:269
  149.5 12.3 %modes.1 = (f32[4,2,3,8192]{3,2,1,0:T(4,128)S(1)}, f32[8,128]{1,0:T(8,128)S(1)}) custom-call(f32[16,32,256]{2,1,0:T(8,128)S(1)} %all-to-all-done.1.gram_ref, f32[16,128]{1,0:T(8,128)S(1)} %reshape.8.start_ref, f32[16,16,8192]{2,1,0:T(8,128)} %all_to_all.10.s_ref), custom_call_target="tpu_custom_call" | custom-call | tf_op jit(solution)/shard_map/modes/pallas_call | solution.py:235
  161.8 1.5 copy.10
  163.3 0.7 copy.11
  (2 shorter events, 0.0 us)
Async XLA Ops:
  0.6 131.5 %copy-start = (f32[64,2,3,32]{0,3,2,1:T(8,128)S(1)}, f32[64,2,3,32]{0,3,2,1:T(8,128)}, u32[]{:S(2)}) copy-start(f32[64,2,3,32]{0,3,2,1:T(8,128)} %param.5) | copy-start | bytes 147460
  0.6 0.9 copy-start.1
  1.6 0.9 copy-start.2
  121.1 28.4 %all-to-all-start.1 = ((f32[16,32,256]{2,1,0:T(8,128)}), f32[16,32,256]{2,1,0:T(8,128)S(1)}, u32[]{:S(2)}, u32[]{:S(2)}) async-start(f32[16,32,256]{2,1,0:T(8,128)} %gram.1), calls=%async_computation.1 | async-start | bytes 1048576 | tf_op jit(solution)/shard_map/all_to_all | solution.py:269

commit v2 on v0

v2 whole, which is shorter than its diff:
```python
import functools
import math

import jax
import jax.numpy as jnp
import numpy as np
from jax import lax
from jax.experimental import pallas as pl
from jax.experimental.pallas import tpu as pltpu
from jax.sharding import PartitionSpec as P

NFFT = 128
FREQS = 64
NB = 32
MODES = 3
ITERS = 2
EPSILON = 1e-06
F32 = jnp.float32
BF16 = jnp.bfloat16
CHUNK = 2048
VMEM_LIMIT = 24 * 1024 * 1024
HBM = pl.BlockSpec(memory_space=pltpu.HBM)
VMEM = pl.BlockSpec(memory_space=pltpu.VMEM)


def dft_table():
    time_ids = np.arange(NFFT)
    phase = np.arange(FREQS)[:, None] * time_ids[None, :] % NFFT
    angles = phase * (2.0 * math.pi / NFFT)
    window = 0.5 - 0.5 * np.cos(time_ids * (2.0 * math.pi / NFFT))
    scaled = window[None, :] * math.sqrt(8.0 / (3.0 * NFFT))
    table = np.stack([np.cos(angles) * scaled, -np.sin(angles) * scaled], axis=1)
    return table.reshape(2 * FREQS, NFFT).astype(np.float32)


def split(value):
    high = value.astype(BF16)
    return high, (value - high.astype(F32)).astype(BF16)


def split3(value):
    high = value.astype(BF16)
    rest = value - high.astype(F32)
    middle = rest.astype(BF16)
    return high, middle, (rest - middle.astype(F32)).astype(BF16)


def dot(left, right):
    return jnp.dot(left, right, preferred_element_type=F32)


def dot_rows(left, right):
    return lax.dot_general(left, right, (((1,), (1,)), ((), ())), preferred_element_type=F32)


def pick_right(value, select):
    high, middle, low = split3(value)
    return dot(high, select) + (dot(middle, select) + dot(low, select))


def pick_left(select, value):
    high, middle, low = split3(value)
    return dot(select, high) + (dot(select, middle) + dot(select, low))


def iota(shape, dim):
    return lax.broadcasted_iota(jnp.int32, shape, dim)


def ones_where(condition):
    return jnp.where(condition, 1.0, 0.0).astype(BF16)


def column_chunks(points):
    size = min(CHUNK, points)
    return [(at, size) for at in range(0, points, size)]


def first_vectors(start, first, bins):
    lanes = NB * bins
    rows, freqs = 2 * MODES * NB, start.shape[3]
    row, col = iota((freqs, lanes), 0), iota((freqs, lanes), 1)
    picked = pick_right(start.reshape(rows, freqs), ones_where(row == first + col % bins))
    picked = jnp.where(iota((rows, lanes), 0) % NB == iota((rows, lanes), 1) // bins, picked, 0.0)
    picked = jnp.sum(picked.reshape(2 * MODES, NB, lanes), axis=1)
    vectors = [(picked[m : m + 1], picked[MODES + m : MODES + m + 1]) for m in range(MODES)]
    vectors = orthonormal(vectors, bin_ones(lanes, bins))
    return jnp.concatenate([stack8(vectors, 0), stack8(vectors, 1)], axis=0)


def transform_kernel(
    owners, table_hbm, x_hbm, start_hbm, out_ref, first_ref, table_ref, x_ref, start_ref, in_sem, small_sem
):
    times, points = x_hbm.shape
    local_blocks = times // NFFT
    chunks = column_chunks(points)

    def fetch(i):
        at, size = chunks[i]
        cols = pl.ds(at, size)
        return pltpu.make_async_copy(x_hbm.at[:, cols], x_ref.at[:, cols], in_sem.at[i])

    table_copy = pltpu.make_async_copy(table_hbm, table_ref, small_sem.at[0])
    start_copy = pltpu.make_async_copy(start_hbm, start_ref, small_sem.at[1])
    table_copy.start()
    start_copy.start()
    for i in range(len(chunks)):
        fetch(i).start()
    bins = FREQS // owners
    start_copy.wait()
    first_ref[...] = first_vectors(start_ref[...], lax.axis_index("tm") * bins, bins)
    table_copy.wait()
    table = table_ref[...].reshape(owners, -1, NFFT)
    blank = jnp.zeros_like(table)
    rows = [
        jnp.concatenate([table if c == b else blank for c in range(local_blocks)], axis=2)
        for b in range(local_blocks)
    ]
    rows = jnp.concatenate(rows, axis=1).reshape(-1, times)
    high, low = split(rows)
    for i, (at, size) in enumerate(chunks):
        fetch(i).wait()
        x_high, x_low = split(x_ref[:, at : at + size])
        out = dot(high, x_high) + (dot(high, x_low) + dot(low, x_high))
        out_ref[:, :, at : at + size] = out.reshape(owners, -1, size)


def transform(snapshots, start, owners):
    times, points = snapshots.shape
    shape = (owners, 2 * FREQS // owners * (times // NFFT), points)
    count = len(column_chunks(points))
    table = pltpu.with_memory_space_constraint(jnp.asarray(dft_table()), pltpu.HBM)
    return pl.pallas_call(
        functools.partial(transform_kernel, owners),
        in_specs=[HBM, HBM, HBM],
        out_specs=[VMEM, VMEM],
        out_shape=[
            pltpu.VMEM(shape, F32),
            jax.ShapeDtypeStruct((16, NB * FREQS // owners), F32),
        ],
        scratch_shapes=[
            pltpu.VMEM((2 * FREQS, NFFT), F32),
            pltpu.VMEM(snapshots.shape, F32),
            pltpu.VMEM(start.shape, F32),
            pltpu.SemaphoreType.DMA((count,)),
            pltpu.SemaphoreType.DMA((2,)),
        ],
        compiler_params=pltpu.CompilerParams(vmem_limit_bytes=24 * 1024 * 1024),
        name="transform",
    )(table, snapshots, start)


def gram_kernel(bins, scale, s_ref, out_ref):
    rows = s_ref.shape[0] * s_ref.shape[1]
    half = rows // 2
    row, col = iota((rows, rows), 0), iota((rows, rows), 1)
    same_bin = (row >> 1) % bins == (col >> 1) % bins
    spread = ones_where(col == (row & 1) * half + (row >> 1))
    row, col = iota((2 * NB, rows), 0), iota((2 * NB, rows), 1)
    fold = ones_where(row == (col & 1) * NB + (col >> 1) // bins)
    same = jnp.zeros((rows, rows), F32)
    cross = jnp.zeros((rows, rows), F32)
    for at, size in column_chunks(s_ref.shape[2]):
        high, low = split(s_ref[:, :, at : at + size].reshape(rows, size))
        same += dot_rows(high, high)
        cross += dot_rows(high, low)
    full = (same + (cross + cross.T)) * scale
    full = jnp.where(same_bin, full, 0.0)
    part = pick_right(pick_left(fold, full), spread)
    real = part[:NB, :half] + part[NB:, half:]
    imag = part[NB:, :half] - part[:NB, half:]
    packed = jnp.where(iota(real.shape, 0) <= iota(real.shape, 1) // bins, real, imag)
    for copy in range(out_ref.shape[0]):
        out_ref[copy] = packed


def partial_gram(spectra, bins, total_points, copies):
    owners, per_owner, points = spectra.shape
    lanes = owners * per_owner // 2
    return pl.pallas_call(
        functools.partial(gram_kernel, bins, 1.0 / (NB * total_points)),
        in_specs=[VMEM],
        out_specs=VMEM,
        out_shape=pltpu.VMEM((copies, NB, lanes), F32),
        compiler_params=pltpu.CompilerParams(vmem_limit_bytes=VMEM_LIMIT),
        name="gram",
    )(spectra)


def bin_ones(lanes, bins):
    return ones_where(iota((lanes, lanes), 0) % bins == iota((lanes, lanes), 1) % bins)


def block_sums(terms, ones):
    stacked = jnp.concatenate(terms + [jnp.zeros((8 - len(terms), ones.shape[0]), F32)], axis=0)
    high, middle, low = split3(stacked)
    sums = dot(high, ones) + (dot(middle, ones) + dot(low, ones))
    return [sums[i : i + 1] for i in range(len(terms))]


def overlap(e, c):
    return [e[0] * c[0] + e[1] * c[1], e[0] * c[1] - e[1] * c[0]]


def orthonormal(vectors, ones):
    left = list(vectors)
    done = []
    while left:
        head = left.pop(0)
        terms = overlap(head, head)[:1]
        for other in left:
            terms = terms + overlap(head, other)
        sums = block_sums(terms, ones)
        norm = jnp.sqrt(sums[0] + EPSILON)
        unit = (head[0] / norm, head[1] / norm)
        for i in range(len(left)):
            real, imag = sums[1 + 2 * i] / norm, sums[2 + 2 * i] / norm
            left[i] = (
                left[i][0] - (unit[0] * real - unit[1] * imag),
                left[i][1] - (unit[0] * imag + unit[1] * real),
            )
        done.append(unit)
    return done


def stack8(vectors, part):
    blank = jnp.zeros((8 - len(vectors), vectors[0][0].shape[1]), F32)
    return jnp.concatenate([v[part] for v in vectors] + [blank], axis=0)


def apply_gram(gram, vectors):
    lanes = vectors[0][0].shape[1]
    both = jnp.concatenate([stack8(vectors, 0), stack8(vectors, 1)], axis=0)
    high, middle, low = split3(both)
    product = dot(high, gram[0]) + (
        (dot(high, gram[1]) + dot(middle, gram[0]))
        + (dot(middle, gram[1]) + (dot(high, gram[2]) + dot(low, gram[0])))
    )
    real = product[:8, :lanes] - product[8:, lanes:]
    imag = product[8:, :lanes] + product[:8, lanes:]
    return [(real[m : m + 1], imag[m : m + 1]) for m in range(MODES)]


def leading(total, start, bins):
    lanes = start.shape[1]
    ones = bin_ones(lanes, bins)
    vectors = [(start[m : m + 1], start[8 + m : 9 + m]) for m in range(MODES)]
    row, col = iota((lanes, NB), 0), iota((lanes, NB), 1)
    packed = pick_left(ones_where(row // bins == col), total)
    row, col = iota(packed.shape, 0), iota(packed.shape, 1)
    packed = jnp.where(row % bins == col % bins, packed, 0.0)
    turned = packed.T
    row, col = row // bins, col // bins
    real = jnp.where(row <= col, packed, turned)
    imag = jnp.where(row > col, packed, jnp.where(row < col, -turned, 0.0))
    gram = split3(jnp.concatenate([real, imag], axis=1))
    for _ in range(ITERS):
        vectors = orthonormal(apply_gram(gram, vectors), ones)
    images = apply_gram(gram, vectors)
    terms = [overlap(v, g)[0] for v, g in zip(vectors, images, strict=True)]
    energies = block_sums(terms, ones)
    weights = [
        (v[0] / jnp.sqrt(NB * e), v[1] / jnp.sqrt(NB * e))
        for v, e in zip(vectors, energies, strict=True)
    ]
    return stack8(weights, 0), stack8(weights, 1), energies


def modes_kernel(bins, grams_ref, start_ref, s_ref, modes_ref, energy_ref):
    rows = s_ref.shape[0] * s_ref.shape[1]
    half = rows // 2
    total = grams_ref[0]
    for i in range(1, grams_ref.shape[0]):
        total = total + grams_ref[i]
    real, imag, energies = leading(total, start_ref[...], bins)
    row, col = iota((half, 2 * rows), 0), iota((half, 2 * rows), 1)
    spread = ones_where(col == 2 * row + jnp.where(col < rows, 0, rows + 1))
    wide = pick_right(jnp.concatenate([real, imag], axis=0), spread)
    to_real = wide[:8, :rows] - wide[8:, rows:]
    to_imag = wide[8:, :rows] + wide[:8, rows:]
    owner = (iota((1, rows), 1) >> 1) % bins
    blank = jnp.zeros((6, rows), F32)
    groups = []
    for k in range(bins):
        for m in range(MODES):
            pair = jnp.concatenate([to_real[m : m + 1], to_imag[m : m + 1]], axis=0)
            groups += [jnp.where(owner == k, pair, 0.0), blank]
    c_both = jnp.concatenate(split(jnp.concatenate(groups, axis=0)), axis=0)
    used = c_both.shape[0] // 2
    for at, size in column_chunks(s_ref.shape[2]):
        s_high, s_low = split(s_ref[:, :, at : at + size].reshape(rows, size))
        both = dot(c_both, s_high)
        out = both[:used] + (both[used:] + dot(c_both[:used], s_low))
        for k in range(bins):
            for m in range(MODES):
                group = (k * MODES + m) * 8
                modes_ref[k, m, :, at : at + size] = out[group : group + 2]
    stacked = jnp.concatenate(energies + [jnp.zeros((8 - MODES, half), F32)], axis=0)
    energy_ref[...] = stacked.T[:bins, :MODES]


def modes_of(grams, start, spectra, bins):
    points = spectra.shape[2]
    return pl.pallas_call(
        functools.partial(modes_kernel, bins),
        in_specs=[VMEM, VMEM, VMEM],
        out_specs=[VMEM, VMEM],
        out_shape=[
            jax.ShapeDtypeStruct((bins, MODES, 2, points), F32),
            jax.ShapeDtypeStruct((bins, MODES), F32),
        ],
        compiler_params=pltpu.CompilerParams(vmem_limit_bytes=VMEM_LIMIT),
        name="modes",
    )(grams, start, spectra)


def on_device(snapshots, start):
    tm_count = lax.axis_size("tm")
    space_count = lax.axis_size("space")
    total_points = snapshots.shape[1] * space_count
    bins = FREQS // tm_count
    snapshots = pltpu.with_memory_space_constraint(snapshots, pltpu.HBM)
    start = pltpu.with_memory_space_constraint(start.transpose(1, 2, 3, 0), pltpu.HBM)
    sent, own = transform(snapshots, start, tm_count)
    spectra = lax.all_to_all(sent, "tm", split_axis=0, concat_axis=0, tiled=True)
    spectra = pltpu.with_memory_space_constraint(spectra, pltpu.VMEM)
    gram = partial_gram(spectra, bins, total_points, space_count)
    grams = lax.all_to_all(gram, "space", split_axis=0, concat_axis=0, tiled=True)
    modes, energies = modes_of(grams, own, spectra, bins)
    return (modes.transpose(0, 2, 1, 3), energies)


def solution(mesh):
    in_specs = (P("tm", "space"), P())
    out_specs = (P("tm", None, None, "space"), P("tm", None))
    return jax.shard_map(
        on_device, mesh=mesh, in_specs=in_specs, out_specs=out_specs, check_vma=False
    )
```

time: 531 us -> 141 us (0.27); the launches traced: 524 us -> 141 us
  waiting for transfers between devices: 422 us -> 0 us
  blocking collectives: 0 us -> 125 us
  matrix products: 50.5 us -> 0 us
  local copies, waits for them, and re-layouts: 18.8 us -> 0 us
  Pallas kernels: 0 us -> 15.7 us
  starting transfers between devices: 14.2 us -> 0 us
  between operations: 14.8 us -> 0.65 us
    psum x1 -> x0, waiting for transfers between devices: 266 us -> none  [on_device(): gram_whole = lax.psum(gram_parts, ('tm', 'space'))]
    all_to_all x2 -> x0, waiting for transfers between devices: 157 us -> none  [the longest x1 146 us: on_device(): lax.all_to_all(snapshots, 'tm', split_axis=1, concat_axis=0, tiled=True)]
    all_to_all x0 -> x2, blocking collectives: none -> 125 us  [the longest x1 102 us: on_device(): lax.all_to_all(sent, 'tm', split_axis=0, concat_axis=0, tiled=True)]
    dot_general x15 -> x0, matrix products: 50.5 us -> none  [the longest x12 23.9 us: batched(): jnp.einsum('fab,fmb->fma', left, right, precision=lax.Precision.HIGHEST)]
    pallas_call x0 -> x3, Pallas kernels: none -> 15.7 us  [the longest x1 7.57 us: transform(): pl.pallas_call(functools.partial(transform_kernel, owners), in_specs=[HBM...]
    all_to_all x2 -> x0, starting transfers between devices: 14.2 us -> none  [the longest x1 7.77 us: on_device(): lax.all_to_all(snapshots, 'tm', split_axis=1, concat_axis=0, tiled=True)]
    all_to_all x2 -> x0, local copies, waits for them, and re-layouts: 9.27 us -> none  [the longest x1 8.02 us: on_device(): lax.all_to_all(snapshots, 'tm', split_axis=1, concat_axis=0, tiled=True)]
    dot_general x14 -> x0, local copies, waits for them, and re-layouts: 6.36 us -> none  [the longest x1 4.86 us: transform(): jnp.einsum('kt,btx->kbx', basis_rows, block_data, precision=lax.Precision...]
  transfers between devices with their start and end apart: 3 -> 0, of which waited for: 3 -> 0; matrix products, arithmetic and copies ran while one was open for 0% -> 0% of each run, Pallas kernels for 0% -> 0%
where the time goes in v2:
time: 141 us
  blocking collectives  125 us (89%)
  Pallas kernels  15.7 us (11%)
    all_to_all x1, blocking collectives, on_device(): lax.all_to_all(sent, 'tm', split_axis=0, concat_axis=0, tiled=True)  102 us
    all_to_all x1, blocking collectives, on_device(): lax.all_to_all(gram, 'space', split_axis=0, concat_axis=0, tiled=True)  22.5 us
    pallas_call x1, Pallas kernels, transform(): pl.pallas_call(functools.partial(transform_kernel, owners), in_specs=[HBM...  7.57 us
    pallas_call x1, Pallas kernels, modes_of(): pl.pallas_call(functools.partial(modes_kernel, bins), in_specs=[VMEM, VME...  5.23 us
    pallas_call x1, Pallas kernels, partial_gram(): pl.pallas_call(functools.partial(gram_kernel, bins, 1.0 / (NB * total_poi...  2.91 us

profile of v2, /device:TPU:1, one launch (start us, length us, event | category | flops | bytes accessed | tf_op | source)
XLA Modules:
  0.0 141.0 jit_solution(1029755047049960631)
XLA Ops:
  0.6 7.6 %transform.1 = (f32[16,16,8192]{2,1,0:T(8,128)S(1)}, f32[16,128]{1,0:T(8,128)S(1)}) custom-call(f32[128,128]{1,0:T(8,128)} %constant.2.clone.table_hbm, f32[256,8192]{1,0:T(8,128)} %x_hbm.1, f32[2,3,32,64]{3,2,1,0:T(8,128)} %bitcast.2), custom_call_target="tpu_custom_call" | custom-call | tf_op jit(solution)/shard_map/transform/pallas_call | solution.py:133
  8.2 102.1 %all_to_all.10.s_ref = f32[16,16,8192]{2,1,0:T(8,128)S(1)} all-to-all(f32[16,16,8192]{2,1,0:T(8,128)S(1)} %get-tuple-element.6), channel_id=1, replica_groups=mesh['tm'=16,'space'=16] {'tm'}, dimensions={0} | all-to-all | bytes 16777216 | tf_op jit(solution)/shard_map/all_to_all | solution.py:325
  110.3 2.9 %gram.1 = f32[16,32,128]{2,1,0:T(8,128)S(1)} custom-call(f32[16,16,8192]{2,1,0:T(8,128)S(1)} %all_to_all.10.s_ref), custom_call_target="tpu_custom_call" | custom-call | tf_op jit(solution)/shard_map/gram/pallas_call | solution.py:180
  113.2 22.5 %all_to_all.11.grams_ref = f32[16,32,128]{2,1,0:T(8,128)S(1)} all-to-all(f32[16,32,128]{2,1,0:T(8,128)S(1)} %gram.1), channel_id=1, replica_groups=mesh['tm'=16,'space'=16] {'space'}, dimensions={0} | all-to-all | bytes 524288 | tf_op jit(solution)/shard_map/all_to_all | solution.py:328
  135.8 5.2 %modes.1 = (f32[4,3,2,8192]{3,2,1,0:T(2,128)}, f32[4,3]{1,0:T(4,128)}) custom-call(f32[16,32,128]{2,1,0:T(8,128)S(1)} %all_to_all.11.grams_ref, f32[16,128]{1,0:T(8,128)S(1)} %get-tuple-element.7.start_ref, f32[16,16,8192]{2,1,0:T(8,128)S(1)} %all_to_all.10.s_ref), custom_call_target="tpu_custom_call" | custom-call | tf_op jit(solution)/shard_map/modes/pallas_call | solution.py:304

commit v3 on v2

--- a/solution.py
+++ b/solution.py
@@ -15,6 +15,8 @@
 MODES = 3
 ITERS = 2
 EPSILON = 1e-06
+BINS = 4
+BLOCKS = 2
 F32 = jnp.float32
 BF16 = jnp.bfloat16
 CHUNK = 2048
@@ -71,9 +73,20 @@
     return jnp.where(condition, 1.0, 0.0).astype(BF16)
 
 
+def row_order(row):
+    pair = (row >> 3) & 1
+    return (row >> 4) * BLOCKS + (((row >> 2) & 1) ^ pair), pair * 2 + ((row >> 1) & 1), row & 1
+
+
 def column_chunks(points):
     size = min(CHUNK, points)
     return [(at, size) for at in range(0, points, size)]
+
+
+def arrival_chunks(points):
+    first = points // 4
+    second = (points - first) // 2
+    return [(0, first), (first, second), (first + second, points - first - second)]
 
 
 def first_vectors(start, first, bins):
@@ -93,7 +106,7 @@
 ):
     times, points = x_hbm.shape
     local_blocks = times // NFFT
-    chunks = column_chunks(points)
+    chunks = arrival_chunks(points)
 
     def fetch(i):
         at, size = chunks[i]
@@ -107,28 +120,32 @@
     for i in range(len(chunks)):
         fetch(i).start()
     bins = FREQS // owners
-    start_copy.wait()
-    first_ref[...] = first_vectors(start_ref[...], lax.axis_index("tm") * bins, bins)
     table_copy.wait()
-    table = table_ref[...].reshape(owners, -1, NFFT)
-    blank = jnp.zeros_like(table)
-    rows = [
-        jnp.concatenate([table if c == b else blank for c in range(local_blocks)], axis=2)
-        for b in range(local_blocks)
-    ]
-    rows = jnp.concatenate(rows, axis=1).reshape(-1, times)
-    high, low = split(rows)
+    table = table_ref[...].reshape(owners, 2, -1, NFFT)
+    table = [table, jnp.concatenate([table[:, 1:], table[:, :1]], axis=1)]
+    table = [split(rows.reshape(-1, NFFT)) for rows in table]
+    wide = [jnp.concatenate([high, low], axis=1) for high, low in table]
     for i, (at, size) in enumerate(chunks):
         fetch(i).wait()
-        x_high, x_low = split(x_ref[:, at : at + size])
-        out = dot(high, x_high) + (dot(high, x_low) + dot(low, x_high))
-        out_ref[:, :, at : at + size] = out.reshape(owners, -1, size)
+        found = []
+        for block in range(BLOCKS):
+            x_high, x_low = split(x_ref[block * NFFT : (block + 1) * NFFT, at : at + size])
+            twice = jnp.concatenate([x_high, x_high], axis=0)
+            out = dot(wide[block], twice) + dot(table[block][0], x_low)
+            found.append(out.reshape(owners, 8, size))
+        upper = iota((owners, 8, size), 1) < 4
+        out_ref[:, :8, at : at + size] = jnp.where(upper, found[0], found[1])
+        out_ref[:, 8:, at : at + size] = jnp.where(upper, found[1], found[0])
+        if i == 1:
+            start_copy.wait()
+            first = lax.axis_index("tm") * bins
+            first_ref[...] = first_vectors(start_ref[...], first, bins)
 
 
 def transform(snapshots, start, owners):
     times, points = snapshots.shape
     shape = (owners, 2 * FREQS // owners * (times // NFFT), points)
-    count = len(column_chunks(points))
+    count = len(arrival_chunks(points))
     table = pltpu.with_memory_space_constraint(jnp.asarray(dft_table()), pltpu.HBM)
     return pl.pallas_call(
         functools.partial(transform_kernel, owners),
@@ -150,38 +167,40 @@
     )(table, snapshots, start)
 
 
-def gram_kernel(bins, scale, s_ref, out_ref):
-    rows = s_ref.shape[0] * s_ref.shape[1]
-    half = rows // 2
-    row, col = iota((rows, rows), 0), iota((rows, rows), 1)
-    same_bin = (row >> 1) % bins == (col >> 1) % bins
-    spread = ones_where(col == (row & 1) * half + (row >> 1))
-    row, col = iota((2 * NB, rows), 0), iota((2 * NB, rows), 1)
-    fold = ones_where(row == (col & 1) * NB + (col >> 1) // bins)
-    same = jnp.zeros((rows, rows), F32)
-    cross = jnp.zeros((rows, rows), F32)
-    for at, size in column_chunks(s_ref.shape[2]):
-        high, low = split(s_ref[:, :, at : at + size].reshape(rows, size))
-        same += dot_rows(high, high)
-        cross += dot_rows(high, low)
-    full = (same + (cross + cross.T)) * scale
-    full = jnp.where(same_bin, full, 0.0)
-    part = pick_right(pick_left(fold, full), spread)
+def gram_kernel(scale, s_ref, out_ref):
+    owners, _, points = s_ref.shape
+    rows, half = owners * 8, NB * BINS
+    sums = [jnp.zeros((2 * rows, rows), F32) for pair in range(2)]
+    for at, size in column_chunks(points):
+        for pair in range(2):
+            value = s_ref[:, pair * 8 : pair * 8 + 8, at : at + size].reshape(rows, size)
+            high, low = split(value)
+            sums[pair] += dot_rows(jnp.concatenate([high, low], axis=0), high)
+    part = jnp.zeros((2 * NB, 2 * half), F32)
+    for pair in range(2):
+        same, cross = sums[pair][:rows], sums[pair][rows:]
+        full = (same + (cross + cross.T)) * scale
+        row, col = iota((rows, rows), 0), iota((rows, rows), 1)
+        full = jnp.where((row >> 1) & 1 == (col >> 1) & 1, full, 0.0)
+        row, col = iota((2 * NB, rows), 0), iota((2 * NB, rows), 1)
+        block, _, which = row_order((col >> 3) * 16 + pair * 8 + (col & 7))
+        fold = ones_where(row == which * NB + block)
+        row, col = iota((rows, 2 * half), 0), iota((rows, 2 * half), 1)
+        block, own_bin, which = row_order((row >> 3) * 16 + pair * 8 + (row & 7))
+        spread = ones_where(col == which * half + block * BINS + own_bin)
+        part += pick_right(pick_left(fold, full), spread)
     real = part[:NB, :half] + part[NB:, half:]
     imag = part[NB:, :half] - part[:NB, half:]
-    packed = jnp.where(iota(real.shape, 0) <= iota(real.shape, 1) // bins, real, imag)
-    for copy in range(out_ref.shape[0]):
-        out_ref[copy] = packed
-
-
-def partial_gram(spectra, bins, total_points, copies):
-    owners, per_owner, points = spectra.shape
-    lanes = owners * per_owner // 2
+    packed = jnp.where(iota(real.shape, 0) <= iota(real.shape, 1) // BINS, real, imag)
+    out_ref[...] = packed
+
+
+def partial_gram(spectra, total_points):
     return pl.pallas_call(
-        functools.partial(gram_kernel, bins, 1.0 / (NB * total_points)),
+        functools.partial(gram_kernel, 1.0 / (NB * total_points)),
         in_specs=[VMEM],
         out_specs=VMEM,
-        out_shape=pltpu.VMEM((copies, NB, lanes), F32),
+        out_shape=pltpu.VMEM((NB, NB * BINS), F32),
         compiler_params=pltpu.CompilerParams(vmem_limit_bytes=VMEM_LIMIT),
         name="gram",
     )(spectra)
@@ -266,19 +285,51 @@
     return stack8(weights, 0), stack8(weights, 1), energies
 
 
-def modes_kernel(bins, grams_ref, start_ref, s_ref, modes_ref, energy_ref):
-    rows = s_ref.shape[0] * s_ref.shape[1]
+def sum_of(refs):
+    total = refs[0][...]
+    for ref in refs[1:]:
+        total = total + ref[...]
+    return total
+
+
+def add_kernel(*refs):
+    refs[-1][...] = sum_of(refs[:-1])
+
+
+def add(parts):
+    return pl.pallas_call(
+        add_kernel,
+        in_specs=[VMEM] * len(parts),
+        out_specs=VMEM,
+        out_shape=pltpu.VMEM(parts[0].shape, F32),
+        compiler_params=pltpu.CompilerParams(vmem_limit_bytes=1024 * 1024),
+        name="add",
+    )(*parts)
+
+
+def exchange(part, offsets):
+    count = lax.axis_size("space")
+    parts = [part]
+    for offset in offsets:
+        pairs = [(i, offset(i, count)) for i in range(count)]
+        parts.append(lax.ppermute(part, "space", pairs))
+    return parts
+
+
+def modes_kernel(bins, *refs):
+    *gram_refs, start_ref, high_ref, low_ref, modes_ref, energy_ref = refs
+    rows, points = high_ref.shape
     half = rows // 2
-    total = grams_ref[0]
-    for i in range(1, grams_ref.shape[0]):
-        total = total + grams_ref[i]
+    total = sum_of(gram_refs)
     real, imag, energies = leading(total, start_ref[...], bins)
     row, col = iota((half, 2 * rows), 0), iota((half, 2 * rows), 1)
-    spread = ones_where(col == 2 * row + jnp.where(col < rows, 0, rows + 1))
+    block, own_bin, which = row_order(col & (rows - 1))
+    chosen = jnp.where(which == col // rows, block * BINS + own_bin, -1)
+    spread = ones_where(row == chosen)
     wide = pick_right(jnp.concatenate([real, imag], axis=0), spread)
     to_real = wide[:8, :rows] - wide[8:, rows:]
     to_imag = wide[8:, :rows] + wide[:8, rows:]
-    owner = (iota((1, rows), 1) >> 1) % bins
+    owner = row_order(iota((1, rows), 1))[1]
     blank = jnp.zeros((6, rows), F32)
     groups = []
     for k in range(bins):
@@ -287,10 +338,9 @@
             groups += [jnp.where(owner == k, pair, 0.0), blank]
     c_both = jnp.concatenate(split(jnp.concatenate(groups, axis=0)), axis=0)
     used = c_both.shape[0] // 2
-    for at, size in column_chunks(s_ref.shape[2]):
-        s_high, s_low = split(s_ref[:, :, at : at + size].reshape(rows, size))
-        both = dot(c_both, s_high)
-        out = both[:used] + (both[used:] + dot(c_both[:used], s_low))
+    for at, size in column_chunks(points):
+        both = dot(c_both, high_ref[:, at : at + size])
+        out = both[:used] + (both[used:] + dot(c_both[:used], low_ref[:, at : at + size]))
         for k in range(bins):
             for m in range(MODES):
                 group = (k * MODES + m) * 8
@@ -299,11 +349,33 @@
     energy_ref[...] = stacked.T[:bins, :MODES]
 
 
-def modes_of(grams, start, spectra, bins):
-    points = spectra.shape[2]
+def halves_kernel(s_ref, high_ref, low_ref):
+    rows = high_ref.shape[0]
+    for at, size in column_chunks(s_ref.shape[2]):
+        high, low = split(s_ref[:, :, at : at + size].reshape(rows, size))
+        high_ref[:, at : at + size] = high
+        low_ref[:, at : at + size] = low
+
+
+def halves_of(spectra):
+    owners, per_owner, points = spectra.shape
+    shape = (owners * per_owner, points)
+    return pl.pallas_call(
+        halves_kernel,
+        in_specs=[VMEM],
+        out_specs=[VMEM, VMEM],
+        out_shape=[pltpu.VMEM(shape, BF16), pltpu.VMEM(shape, BF16)],
+        compiler_params=pltpu.CompilerParams(vmem_limit_bytes=8 * 1024 * 1024),
+        cost_estimate=pl.CostEstimate(flops=10**7, bytes_accessed=10**6, transcendentals=0),
+        name="halves",
+    )(spectra)
+
+
+def modes_of(grams, start, high, low, bins):
+    points = high.shape[1]
     return pl.pallas_call(
         functools.partial(modes_kernel, bins),
-        in_specs=[VMEM, VMEM, VMEM],
+        in_specs=[VMEM] * (len(grams) + 3),
         out_specs=[VMEM, VMEM],
         out_shape=[
             jax.ShapeDtypeStruct((bins, MODES, 2, points), F32),
@@ -311,7 +383,7 @@
         ],
         compiler_params=pltpu.CompilerParams(vmem_limit_bytes=VMEM_LIMIT),
         name="modes",
-    )(grams, start, spectra)
+    )(*grams, start, high, low)
 
 
 def on_device(snapshots, start):
@@ -324,9 +396,10 @@
     sent, own = transform(snapshots, start, tm_count)
     spectra = lax.all_to_all(sent, "tm", split_axis=0, concat_axis=0, tiled=True)
     spectra = pltpu.with_memory_space_constraint(spectra, pltpu.VMEM)
-    gram = partial_gram(spectra, bins, total_points, space_count)
-    grams = lax.all_to_all(gram, "space", split_axis=0, concat_axis=0, tiled=True)
-    modes, energies = modes_of(grams, own, spectra, bins)
+    gram = partial_gram(spectra, total_points)
+    near = add(exchange(gram, [lambda i, n, k=k: i ^ k for k in (1, 2, 3)]))
+    grams = exchange(near, [lambda i, n, k=k: (i + 4 * k) % n for k in (1, 3, 2)])
+    modes, energies = modes_of(grams, own, *halves_of(spectra), bins)
     return (modes.transpose(0, 2, 1, 3), energies)
 
 

time: 141 us -> 134 us (0.950)
  blocking collectives: 125 us -> 102 us
  starting transfers between devices: 0 us -> 13.5 us
  waiting for transfers between devices: 0 us -> 3.24 us
  Pallas kernels: 15.7 us -> 14.2 us
    all_to_all x1 -> x0, blocking collectives: 22.5 us -> none  [on_device(): lax.all_to_all(gram, 'space', split_axis=0, concat_axis=0, tiled=True)]
    ppermute x0 -> x6, starting transfers between devices: none -> 13.5 us  [exchange(): parts.append(lax.ppermute(part, 'space', pairs))]
    ppermute x0 -> x6, waiting for transfers between devices: none -> 3.24 us  [exchange(): parts.append(lax.ppermute(part, 'space', pairs))]
    pallas_call x1, Pallas kernels: 7.57 us -> 5.33 us  [transform(): pl.pallas_call(functools.partial(transform_kernel, owners), in_specs=[HBM...]
    pallas_call x2 -> x4, Pallas kernels: 8.14 us -> 8.86 us  [the longest x1 4.87 us: modes_of(): pl.pallas_call(functools.partial(modes_kernel, bins), in_specs=[VMEM] * (...]
  transfers between devices with their start and end apart: 0 -> 6, of which waited for: 0 -> 3; matrix products, arithmetic and copies ran while one was open for 0% -> 0% of each run, Pallas kernels for 0% -> 1%
where the time goes in v3:
time: 134 us
  blocking collectives  102 us (76%)
  Pallas kernels  14.2 us (11%)
  starting transfers between devices  13.5 us (10%)
  waiting for transfers between devices  3.24 us (2%)
    all_to_all x1, blocking collectives, on_device(): lax.all_to_all(sent, 'tm', split_axis=0, concat_axis=0, tiled=True)  102 us
    ppermute x6, starting transfers between devices, exchange(): parts.append(lax.ppermute(part, 'space', pairs))  13.5 us
    pallas_call x1, Pallas kernels, transform(): pl.pallas_call(functools.partial(transform_kernel, owners), in_specs=[HBM...  5.33 us
    pallas_call x1, Pallas kernels, modes_of(): pl.pallas_call(functools.partial(modes_kernel, bins), in_specs=[VMEM] * (...  4.87 us
    ppermute x6, waiting for transfers between devices, exchange(): parts.append(lax.ppermute(part, 'space', pairs))  3.24 us
    pallas_call x1, Pallas kernels, partial_gram(): pl.pallas_call(functools.partial(gram_kernel, 1.0 / (NB * total_points)),...  2.8 us
  transfers between devices with their start and end apart: 6, of which 3 were waited for; matrix products, arithmetic and copies ran while one was open for 0% of the time, Pallas kernels for 1%

profile of v3, /device:TPU:1, one launch (start us, length us, event | category | flops | bytes accessed | tf_op | source)
XLA Modules:
  0.0 133.7 jit_solution(8287590832076010544)
XLA Ops:
  0.6 5.3 %transform.1 = (f32[16,16,8192]{2,1,0:T(8,128)S(1)}, f32[16,128]{1,0:T(8,128)S(1)}) custom-call(f32[128,128]{1,0:T(8,128)} %constant.2.clone.table_hbm, f32[256,8192]{1,0:T(8,128)} %x_hbm.1, f32[2,3,32,64]{3,2,1,0:T(8,128)} %bitcast.2), custom_call_target="tpu_custom_call" | custom-call | tf_op jit(solution)/shard_map/transform/pallas_call | solution.py:150
  6.0 102.1 %all_to_all.5.s_ref = f32[16,16,8192]{2,1,0:T(8,128)S(1)} all-to-all(f32[16,16,8192]{2,1,0:T(8,128)S(1)} %get-tuple-element.8), channel_id=1, replica_groups=mesh['tm'=16,'space'=16] {'tm'}, dimensions={0} | all-to-all | bytes 16777216 | tf_op jit(solution)/shard_map/all_to_all | solution.py:397
  108.1 2.8 %gram.1.refs_0_ = f32[32,128]{1,0:T(8,128)S(1)} custom-call(f32[16,16,8192]{2,1,0:T(8,128)S(1)} %all_to_all.5.s_ref), custom_call_target="tpu_custom_call" | custom-call | tf_op jit(solution)/shard_map/gram/pallas_call | solution.py:199
  110.9 4.2 %collective-permute-start.2 = (f32[32,128]{1,0:T(8,128)S(1)}, f32[32,128]{1,0:T(8,128)S(1)}, u32[]{:S(2)}, u32[]{:S(2)}) collective-permute-start(f32[32,128]{1,0:T(8,128)S(1)} %gram.1.refs_0_), channel_id=1, source_target_pairs={{0,3},{1,2},{2,1},{3,0},{4,7},{5,6},{6,5},{7,4},{8,11},{9,10},{10,... | collective-permute-start | bytes 49160 | tf_op jit(solution)/shard_map/ppermute | solution.py:315
  115.0 0.0 collective-permute-start.1
  115.0 0.5 collective-permute-start
  115.5 0.9 collective-permute-done.2.refs_3_
  116.5 1.2 collective-permute-done.1.refs_2_
  117.6 0.0 collective-permute-done.refs_1_
  117.6 6.4 %collective-permute-start.5 = (f32[32,128]{1,0:T(8,128)S(1)}, f32[32,128]{1,0:T(8,128)S(1)}, u32[]{:S(2)}, u32[]{:S(2)}) collective-permute-start(f32[32,128]{1,0:T(8,128)S(1)} %add.1.refs_0_), channel_id=1, source_target_pairs={{0,8},{1,9},{2,10},{3,11},{4,12},{5,13},{6,14},{7,15},{8,0},{9,1},... | collective-permute-start | bytes 49160 | tf_op jit(solution)/shard_map/ppermute | solution.py:315
  124.1 0.0 collective-permute-start.4
  124.1 2.4 %collective-permute-start.3 = (f32[32,128]{1,0:T(8,128)S(1)}, f32[32,128]{1,0:T(8,128)S(1)}, u32[]{:S(2)}, u32[]{:S(2)}) collective-permute-start(f32[32,128]{1,0:T(8,128)S(1)} %add.1.refs_0_), channel_id=1, source_target_pairs={{0,4},{1,5},{2,6},{3,7},{4,8},{5,9},{6,10},{7,11},{8,12},{9,13},{1... | collective-permute-start | bytes 49160 | tf_op jit(solution)/shard_map/ppermute | solution.py:315
  126.4 1.2 halves.1
  127.6 0.0 collective-permute-done.5.refs_3_
  127.6 0.0 collective-permute-done.4.refs_2_
  127.6 1.1 collective-permute-done.3.refs_1_
  128.8 4.9 %modes.1 = (f32[4,3,2,8192]{3,2,1,0:T(2,128)}, f32[4,3]{1,0:T(4,128)}) custom-call(f32[32,128]{1,0:T(8,128)S(1)} %add.1.refs_0_, f32[32,128]{1,0:T(8,128)S(1)} %collective-permute-done.3.refs_1_, f32[32,128]{1,0:T(8,128)S(1)} %collective-permute-done.4.refs_2_, f32[32,128]{1,0:T(8,128)S(1)} %collective-permute-done.5.refs_3_, ...), custom_call_target="tpu_custom_call" | custom-call | tf_op jit(solution)/shard_map/modes/pallas_call | solution.py:376
  (1 shorter events, 0.0 us)
Async XLA Ops:
  110.9 5.6 %collective-permute-start.2 = (f32[32,128]{1,0:T(8,128)S(1)}, f32[32,128]{1,0:T(8,128)S(1)}, u32[]{:S(2)}, u32[]{:S(2)}) collective-permute-start(f32[32,128]{1,0:T(8,128)S(1)} %gram.1.refs_0_), channel_id=1, source_target_pairs={{0,3},{1,2},{2,1},{3,0},{4,7},{5,6},{6,5},{7,4},{8,11},{9,10},{10,... | collective-permute-start | bytes 49160 | tf_op jit(solution)/shard_map/ppermute | solution.py:315
  115.0 2.6 %collective-permute-start.1 = (f32[32,128]{1,0:T(8,128)S(1)}, f32[32,128]{1,0:T(8,128)S(1)}, u32[]{:S(2)}, u32[]{:S(2)}) collective-permute-start(f32[32,128]{1,0:T(8,128)S(1)} %gram.1.refs_0_), channel_id=1, source_target_pairs={{0,2},{1,3},{2,0},{3,1},{4,6},{5,7},{6,4},{7,5},{8,10},{9,11},{10,... | collective-permute-start | bytes 49160 | tf_op jit(solution)/shard_map/ppermute | solution.py:315
  115.0 2.6 %collective-permute-start = (f32[32,128]{1,0:T(8,128)S(1)}, f32[32,128]{1,0:T(8,128)S(1)}, u32[]{:S(2)}, u32[]{:S(2)}) collective-permute-start(f32[32,128]{1,0:T(8,128)S(1)} %gram.1.refs_0_), channel_id=1, source_target_pairs={{0,1},{1,0},{2,3},{3,2},{4,5},{5,4},{6,7},{7,6},{8,9},{9,8},{10,11... | collective-permute-start | bytes 49160 | tf_op jit(solution)/shard_map/ppermute | solution.py:315
  117.6 10.0 %collective-permute-start.5 = (f32[32,128]{1,0:T(8,128)S(1)}, f32[32,128]{1,0:T(8,128)S(1)}, u32[]{:S(2)}, u32[]{:S(2)}) collective-permute-start(f32[32,128]{1,0:T(8,128)S(1)} %add.1.refs_0_), channel_id=1, source_target_pairs={{0,8},{1,9},{2,10},{3,11},{4,12},{5,13},{6,14},{7,15},{8,0},{9,1},... | collective-permute-start | bytes 49160 | tf_op jit(solution)/shard_map/ppermute | solution.py:315
  124.1 3.6 %collective-permute-start.4 = (f32[32,128]{1,0:T(8,128)S(1)}, f32[32,128]{1,0:T(8,128)S(1)}, u32[]{:S(2)}, u32[]{:S(2)}) collective-permute-start(f32[32,128]{1,0:T(8,128)S(1)} %add.1.refs_0_), channel_id=1, source_target_pairs={{0,12},{1,13},{2,14},{3,15},{4,0},{5,1},{6,2},{7,3},{8,4},{9,5},{1... | collective-permute-start | bytes 49160 | tf_op jit(solution)/shard_map/ppermute | solution.py:315
  124.1 4.7 %collective-permute-start.3 = (f32[32,128]{1,0:T(8,128)S(1)}, f32[32,128]{1,0:T(8,128)S(1)}, u32[]{:S(2)}, u32[]{:S(2)}) collective-permute-start(f32[32,128]{1,0:T(8,128)S(1)} %add.1.refs_0_), channel_id=1, source_target_pairs={{0,4},{1,5},{2,6},{3,7},{4,8},{5,9},{6,10},{7,11},{8,12},{9,13},{1... | collective-permute-start | bytes 49160 | tf_op jit(solution)/shard_map/ppermute | solution.py:315

commit v4 on v3

--- a/solution.py
+++ b/solution.py
@@ -56,8 +56,9 @@
 
 
 def pick_right(value, select):
-    high, middle, low = split3(value)
-    return dot(high, select) + (dot(middle, select) + dot(low, select))
+    rows = value.shape[0]
+    parts = dot(jnp.concatenate(split3(value), axis=0), select)
+    return parts[:rows] + (parts[rows : 2 * rows] + parts[2 * rows :])
 
 
 def pick_left(select, value):
@@ -211,9 +212,8 @@
 
 
 def block_sums(terms, ones):
-    stacked = jnp.concatenate(terms + [jnp.zeros((8 - len(terms), ones.shape[0]), F32)], axis=0)
-    high, middle, low = split3(stacked)
-    sums = dot(high, ones) + (dot(middle, ones) + dot(low, ones))
+    blank = jnp.zeros((16 - len(terms), ones.shape[0]), F32)
+    sums = pick_right(jnp.concatenate(terms + [blank], axis=0), ones)
     return [sums[i : i + 1] for i in range(len(terms))]
 
 
@@ -250,11 +250,9 @@
 def apply_gram(gram, vectors):
     lanes = vectors[0][0].shape[1]
     both = jnp.concatenate([stack8(vectors, 0), stack8(vectors, 1)], axis=0)
-    high, middle, low = split3(both)
-    product = dot(high, gram[0]) + (
-        (dot(high, gram[1]) + dot(middle, gram[0]))
-        + (dot(middle, gram[1]) + (dot(high, gram[2]) + dot(low, gram[0])))
-    )
+    parts = jnp.concatenate(split3(both), axis=0)
+    first, second, third = dot(parts, gram[0]), dot(parts[:32], gram[1]), dot(parts[:16], gram[2])
+    product = first[:16] + ((first[16:32] + second[:16]) + (first[32:] + (second[16:] + third)))
     real = product[:8, :lanes] - product[8:, lanes:]
     imag = product[8:, :lanes] + product[:8, lanes:]
     return [(real[m : m + 1], imag[m : m + 1]) for m in range(MODES)]

time: 134 us -> 134 us (level)
  no operation moved by 1% of the time
where the time goes in v4:
time: 134 us; the launch traced here: 133 us
  blocking collectives  102 us (76%)
  Pallas kernels  13.9 us (10%)
  starting transfers between devices  13.5 us (10%)
  waiting for transfers between devices  3.24 us (2%)
    all_to_all x1, blocking collectives, on_device(): lax.all_to_all(sent, 'tm', split_axis=0, concat_axis=0, tiled=True)  102 us
    ppermute x6, starting transfers between devices, exchange(): parts.append(lax.ppermute(part, 'space', pairs))  13.5 us
    pallas_call x1, Pallas kernels, transform(): pl.pallas_call(functools.partial(transform_kernel, owners), in_specs=[HBM...  5.45 us
    pallas_call x1, Pallas kernels, modes_of(): pl.pallas_call(functools.partial(modes_kernel, bins), in_specs=[VMEM] * (...  4.47 us
    ppermute x6, waiting for transfers between devices, exchange(): parts.append(lax.ppermute(part, 'space', pairs))  3.24 us
    pallas_call x1, Pallas kernels, partial_gram(): pl.pallas_call(functools.partial(gram_kernel, 1.0 / (NB * total_points)),...  2.79 us
  transfers between devices with their start and end apart: 6, of which 3 were waited for; matrix products, arithmetic and copies ran while one was open for 0% of the time, Pallas kernels for 1%

profile of v4, /device:TPU:1, one launch (start us, length us, event | category | flops | bytes accessed | tf_op | source)
XLA Modules:
  0.0 133.4 jit_solution(9505288109307657507)
XLA Ops:
  0.6 5.5 %transform.1 = (f32[16,16,8192]{2,1,0:T(8,128)S(1)}, f32[16,128]{1,0:T(8,128)S(1)}) custom-call(f32[128,128]{1,0:T(8,128)} %constant.2.clone.table_hbm, f32[256,8192]{1,0:T(8,128)} %x_hbm.1, f32[2,3,32,64]{3,2,1,0:T(8,128)} %bitcast.2), custom_call_target="tpu_custom_call" | custom-call | tf_op jit(solution)/shard_map/transform/pallas_call | solution.py:151
  6.1 102.1 %all_to_all.5.s_ref = f32[16,16,8192]{2,1,0:T(8,128)S(1)} all-to-all(f32[16,16,8192]{2,1,0:T(8,128)S(1)} %get-tuple-element.8), channel_id=1, replica_groups=mesh['tm'=16,'space'=16] {'tm'}, dimensions={0} | all-to-all | bytes 16777216 | tf_op jit(solution)/shard_map/all_to_all | solution.py:395
  108.2 2.8 %gram.1.refs_0_ = f32[32,128]{1,0:T(8,128)S(1)} custom-call(f32[16,16,8192]{2,1,0:T(8,128)S(1)} %all_to_all.5.s_ref), custom_call_target="tpu_custom_call" | custom-call | tf_op jit(solution)/shard_map/gram/pallas_call | solution.py:200
  111.0 4.2 %collective-permute-start.2 = (f32[32,128]{1,0:T(8,128)S(1)}, f32[32,128]{1,0:T(8,128)S(1)}, u32[]{:S(2)}, u32[]{:S(2)}) collective-permute-start(f32[32,128]{1,0:T(8,128)S(1)} %gram.1.refs_0_), channel_id=1, source_target_pairs={{0,3},{1,2},{2,1},{3,0},{4,7},{5,6},{6,5},{7,4},{8,11},{9,10},{10,... | collective-permute-start | bytes 49160 | tf_op jit(solution)/shard_map/ppermute | solution.py:313
  115.2 0.0 collective-permute-start.1
  115.2 0.5 collective-permute-start
  115.7 0.9 collective-permute-done.2.refs_3_
  116.6 1.2 collective-permute-done.1.refs_2_
  117.8 0.0 collective-permute-done.refs_1_
  117.8 6.4 %collective-permute-start.5 = (f32[32,128]{1,0:T(8,128)S(1)}, f32[32,128]{1,0:T(8,128)S(1)}, u32[]{:S(2)}, u32[]{:S(2)}) collective-permute-start(f32[32,128]{1,0:T(8,128)S(1)} %add.1.refs_0_), channel_id=1, source_target_pairs={{0,8},{1,9},{2,10},{3,11},{4,12},{5,13},{6,14},{7,15},{8,0},{9,1},... | collective-permute-start | bytes 49160 | tf_op jit(solution)/shard_map/ppermute | solution.py:313
  124.2 0.0 collective-permute-start.4
  124.2 2.4 %collective-permute-start.3 = (f32[32,128]{1,0:T(8,128)S(1)}, f32[32,128]{1,0:T(8,128)S(1)}, u32[]{:S(2)}, u32[]{:S(2)}) collective-permute-start(f32[32,128]{1,0:T(8,128)S(1)} %add.1.refs_0_), channel_id=1, source_target_pairs={{0,4},{1,5},{2,6},{3,7},{4,8},{5,9},{6,10},{7,11},{8,12},{9,13},{1... | collective-permute-start | bytes 49160 | tf_op jit(solution)/shard_map/ppermute | solution.py:313
  126.6 1.2 halves.1
  127.7 0.0 collective-permute-done.5.refs_3_
  127.8 0.0 collective-permute-done.4.refs_2_
  127.8 1.1 collective-permute-done.3.refs_1_
  128.9 4.5 %modes.1 = (f32[4,3,2,8192]{3,2,1,0:T(2,128)}, f32[4,3]{1,0:T(4,128)}) custom-call(f32[32,128]{1,0:T(8,128)S(1)} %add.1.refs_0_, f32[32,128]{1,0:T(8,128)S(1)} %collective-permute-done.3.refs_1_, f32[32,128]{1,0:T(8,128)S(1)} %collective-permute-done.4.refs_2_, f32[32,128]{1,0:T(8,128)S(1)} %collective-permute-done.5.refs_3_, ...), custom_call_target="tpu_custom_call" | custom-call | tf_op jit(solution)/shard_map/modes/pallas_call | solution.py:374
  (1 shorter events, 0.0 us)
Async XLA Ops:
  111.0 5.6 %collective-permute-start.2 = (f32[32,128]{1,0:T(8,128)S(1)}, f32[32,128]{1,0:T(8,128)S(1)}, u32[]{:S(2)}, u32[]{:S(2)}) collective-permute-start(f32[32,128]{1,0:T(8,128)S(1)} %gram.1.refs_0_), channel_id=1, source_target_pairs={{0,3},{1,2},{2,1},{3,0},{4,7},{5,6},{6,5},{7,4},{8,11},{9,10},{10,... | collective-permute-start | bytes 49160 | tf_op jit(solution)/shard_map/ppermute | solution.py:313
  115.2 2.6 %collective-permute-start.1 = (f32[32,128]{1,0:T(8,128)S(1)}, f32[32,128]{1,0:T(8,128)S(1)}, u32[]{:S(2)}, u32[]{:S(2)}) collective-permute-start(f32[32,128]{1,0:T(8,128)S(1)} %gram.1.refs_0_), channel_id=1, source_target_pairs={{0,2},{1,3},{2,0},{3,1},{4,6},{5,7},{6,4},{7,5},{8,10},{9,11},{10,... | collective-permute-start | bytes 49160 | tf_op jit(solution)/shard_map/ppermute | solution.py:313
  115.2 2.6 %collective-permute-start = (f32[32,128]{1,0:T(8,128)S(1)}, f32[32,128]{1,0:T(8,128)S(1)}, u32[]{:S(2)}, u32[]{:S(2)}) collective-permute-start(f32[32,128]{1,0:T(8,128)S(1)} %gram.1.refs_0_), channel_id=1, source_target_pairs={{0,1},{1,0},{2,3},{3,2},{4,5},{5,4},{6,7},{7,6},{8,9},{9,8},{10,11... | collective-permute-start | bytes 49160 | tf_op jit(solution)/shard_map/ppermute | solution.py:313
  117.8 10.0 %collective-permute-start.5 = (f32[32,128]{1,0:T(8,128)S(1)}, f32[32,128]{1,0:T(8,128)S(1)}, u32[]{:S(2)}, u32[]{:S(2)}) collective-permute-start(f32[32,128]{1,0:T(8,128)S(1)} %add.1.refs_0_), channel_id=1, source_target_pairs={{0,8},{1,9},{2,10},{3,11},{4,12},{5,13},{6,14},{7,15},{8,0},{9,1},... | collective-permute-start | bytes 49160 | tf_op jit(solution)/shard_map/ppermute | solution.py:313
  124.2 3.6 %collective-permute-start.4 = (f32[32,128]{1,0:T(8,128)S(1)}, f32[32,128]{1,0:T(8,128)S(1)}, u32[]{:S(2)}, u32[]{:S(2)}) collective-permute-start(f32[32,128]{1,0:T(8,128)S(1)} %add.1.refs_0_), channel_id=1, source_target_pairs={{0,12},{1,13},{2,14},{3,15},{4,0},{5,1},{6,2},{7,3},{8,4},{9,5},{1... | collective-permute-start | bytes 49160 | tf_op jit(solution)/shard_map/ppermute | solution.py:313
  124.2 4.7 %collective-permute-start.3 = (f32[32,128]{1,0:T(8,128)S(1)}, f32[32,128]{1,0:T(8,128)S(1)}, u32[]{:S(2)}, u32[]{:S(2)}) collective-permute-start(f32[32,128]{1,0:T(8,128)S(1)} %add.1.refs_0_), channel_id=1, source_target_pairs={{0,4},{1,5},{2,6},{3,7},{4,8},{5,9},{6,10},{7,11},{8,12},{9,13},{1... | collective-permute-start | bytes 49160 | tf_op jit(solution)/shard_map/ppermute | solution.py:313

commit v5 on v4

--- a/solution.py
+++ b/solution.py
@@ -75,8 +75,7 @@
 
 
 def row_order(row):
-    pair = (row >> 3) & 1
-    return (row >> 4) * BLOCKS + (((row >> 2) & 1) ^ pair), pair * 2 + ((row >> 1) & 1), row & 1
+    return row >> 3, (row >> 1) & 3, row & 1
 
 
 def column_chunks(points):
@@ -122,21 +121,16 @@
         fetch(i).start()
     bins = FREQS // owners
     table_copy.wait()
-    table = table_ref[...].reshape(owners, 2, -1, NFFT)
-    table = [table, jnp.concatenate([table[:, 1:], table[:, :1]], axis=1)]
-    table = [split(rows.reshape(-1, NFFT)) for rows in table]
-    wide = [jnp.concatenate([high, low], axis=1) for high, low in table]
+    high, middle, low = split3(table_ref[...])
+    wide = jnp.concatenate([high, middle, low, high, middle, high], axis=1)
     for i, (at, size) in enumerate(chunks):
         fetch(i).wait()
-        found = []
+        x = x_ref[:, at : at + size]
+        x_high, x_middle, x_low = split3(jnp.concatenate([x[:NFFT], x[NFFT:]], axis=1))
+        out = dot(wide, jnp.concatenate([x_high, x_high, x_high, x_middle, x_middle, x_low], axis=0))
         for block in range(BLOCKS):
-            x_high, x_low = split(x_ref[block * NFFT : (block + 1) * NFFT, at : at + size])
-            twice = jnp.concatenate([x_high, x_high], axis=0)
-            out = dot(wide[block], twice) + dot(table[block][0], x_low)
-            found.append(out.reshape(owners, 8, size))
-        upper = iota((owners, 8, size), 1) < 4
-        out_ref[:, :8, at : at + size] = jnp.where(upper, found[0], found[1])
-        out_ref[:, 8:, at : at + size] = jnp.where(upper, found[1], found[0])
+            rows, cols = slice(block * 8, block * 8 + 8), slice(block * size, block * size + size)
+            out_ref[:, rows, at : at + size] = out[:, cols].reshape(owners, 8, size)
         if i == 1:
             start_copy.wait()
             first = lax.axis_index("tm") * bins
@@ -169,27 +163,23 @@
 
 
 def gram_kernel(scale, s_ref, out_ref):
-    owners, _, points = s_ref.shape
-    rows, half = owners * 8, NB * BINS
-    sums = [jnp.zeros((2 * rows, rows), F32) for pair in range(2)]
+    points = s_ref.shape[2]
+    rows, half = 2 * NB * BINS, NB * BINS
+    sums = jnp.zeros((2 * rows, rows), F32)
     for at, size in column_chunks(points):
-        for pair in range(2):
-            value = s_ref[:, pair * 8 : pair * 8 + 8, at : at + size].reshape(rows, size)
-            high, low = split(value)
-            sums[pair] += dot_rows(jnp.concatenate([high, low], axis=0), high)
-    part = jnp.zeros((2 * NB, 2 * half), F32)
-    for pair in range(2):
-        same, cross = sums[pair][:rows], sums[pair][rows:]
-        full = (same + (cross + cross.T)) * scale
-        row, col = iota((rows, rows), 0), iota((rows, rows), 1)
-        full = jnp.where((row >> 1) & 1 == (col >> 1) & 1, full, 0.0)
-        row, col = iota((2 * NB, rows), 0), iota((2 * NB, rows), 1)
-        block, _, which = row_order((col >> 3) * 16 + pair * 8 + (col & 7))
-        fold = ones_where(row == which * NB + block)
-        row, col = iota((rows, 2 * half), 0), iota((rows, 2 * half), 1)
-        block, own_bin, which = row_order((row >> 3) * 16 + pair * 8 + (row & 7))
-        spread = ones_where(col == which * half + block * BINS + own_bin)
-        part += pick_right(pick_left(fold, full), spread)
+        high, low = split(s_ref[:, :, at : at + size].reshape(rows, size))
+        sums += dot_rows(jnp.concatenate([high, low], axis=0), high)
+    cross = sums[rows:]
+    full = (sums[:rows] + (cross + cross.T)) * scale
+    row, col = iota((rows, rows), 0), iota((rows, rows), 1)
+    full = jnp.where(row_order(row)[1] == row_order(col)[1], full, 0.0)
+    row, col = iota((2 * NB, rows), 0), iota((2 * NB, rows), 1)
+    block, _, which = row_order(col)
+    fold = ones_where(row == which * NB + block)
+    row, col = iota((rows, 2 * half), 0), iota((rows, 2 * half), 1)
+    block, own_bin, which = row_order(row)
+    spread = ones_where(col == which * half + block * BINS + own_bin)
+    part = pick_right(pick_left(fold, full), spread)
     real = part[:NB, :half] + part[NB:, half:]
     imag = part[NB:, :half] - part[:NB, half:]
     packed = jnp.where(iota(real.shape, 0) <= iota(real.shape, 1) // BINS, real, imag)

time: 134 us -> 134 us (level)
  no operation moved by 1% of the time
where the time goes in v5:
time: 134 us
  blocking collectives  102 us (76%)
  Pallas kernels  14.7 us (11%)
  starting transfers between devices  13.5 us (10%)
  waiting for transfers between devices  3.24 us (2%)
    all_to_all x1, blocking collectives, on_device(): lax.all_to_all(sent, 'tm', split_axis=0, concat_axis=0, tiled=True)  102 us
    ppermute x6, starting transfers between devices, exchange(): parts.append(lax.ppermute(part, 'space', pairs))  13.5 us
    pallas_call x1, Pallas kernels, transform(): pl.pallas_call(functools.partial(transform_kernel, owners), in_specs=[HBM...  6.13 us
    pallas_call x1, Pallas kernels, modes_of(): pl.pallas_call(functools.partial(modes_kernel, bins), in_specs=[VMEM] * (...  4.47 us
    ppermute x6, waiting for transfers between devices, exchange(): parts.append(lax.ppermute(part, 'space', pairs))  3.24 us
    pallas_call x1, Pallas kernels, partial_gram(): pl.pallas_call(functools.partial(gram_kernel, 1.0 / (NB * total_points)),...  2.92 us
  transfers between devices with their start and end apart: 6, of which 3 were waited for; matrix products, arithmetic and copies ran while one was open for 0% of the time, Pallas kernels for 1%

profile of v5, /device:TPU:1, one launch (start us, length us, event | category | flops | bytes accessed | tf_op | source)
XLA Modules:
  0.0 134.2 jit_solution(17541363396596225578)
XLA Ops:
  0.6 6.1 %transform.1 = (f32[16,16,8192]{2,1,0:T(8,128)S(1)}, f32[16,128]{1,0:T(8,128)S(1)}) custom-call(f32[128,128]{1,0:T(8,128)} %constant.2.clone.table_hbm, f32[256,8192]{1,0:T(8,128)} %x_hbm.1, f32[2,3,32,64]{3,2,1,0:T(8,128)} %bitcast.2), custom_call_target="tpu_custom_call" | custom-call | tf_op jit(solution)/shard_map/transform/pallas_call | solution.py:145
  6.8 102.1 %all_to_all.5.s_ref = f32[16,16,8192]{2,1,0:T(8,128)S(1)} all-to-all(f32[16,16,8192]{2,1,0:T(8,128)S(1)} %get-tuple-element.8), channel_id=1, replica_groups=mesh['tm'=16,'space'=16] {'tm'}, dimensions={0} | all-to-all | bytes 16777216 | tf_op jit(solution)/shard_map/all_to_all | solution.py:385
  108.9 2.9 %gram.1.refs_0_ = f32[32,128]{1,0:T(8,128)S(1)} custom-call(f32[16,16,8192]{2,1,0:T(8,128)S(1)} %all_to_all.5.s_ref), custom_call_target="tpu_custom_call" | custom-call | tf_op jit(solution)/shard_map/gram/pallas_call | solution.py:190
  111.8 4.2 %collective-permute-start.2 = (f32[32,128]{1,0:T(8,128)S(1)}, f32[32,128]{1,0:T(8,128)S(1)}, u32[]{:S(2)}, u32[]{:S(2)}) collective-permute-start(f32[32,128]{1,0:T(8,128)S(1)} %gram.1.refs_0_), channel_id=1, source_target_pairs={{0,3},{1,2},{2,1},{3,0},{4,7},{5,6},{6,5},{7,4},{8,11},{9,10},{10,... | collective-permute-start | bytes 49160 | tf_op jit(solution)/shard_map/ppermute | solution.py:303
  116.0 0.0 collective-permute-start.1
  116.0 0.5 collective-permute-start
  116.5 0.9 collective-permute-done.2.refs_3_
  117.4 1.2 collective-permute-done.1.refs_2_
  118.6 0.0 collective-permute-done.refs_1_
  118.6 6.4 %collective-permute-start.5 = (f32[32,128]{1,0:T(8,128)S(1)}, f32[32,128]{1,0:T(8,128)S(1)}, u32[]{:S(2)}, u32[]{:S(2)}) collective-permute-start(f32[32,128]{1,0:T(8,128)S(1)} %add.1.refs_0_), channel_id=1, source_target_pairs={{0,8},{1,9},{2,10},{3,11},{4,12},{5,13},{6,14},{7,15},{8,0},{9,1},... | collective-permute-start | bytes 49160 | tf_op jit(solution)/shard_map/ppermute | solution.py:303
  125.0 0.0 collective-permute-start.4
  125.0 2.4 %collective-permute-start.3 = (f32[32,128]{1,0:T(8,128)S(1)}, f32[32,128]{1,0:T(8,128)S(1)}, u32[]{:S(2)}, u32[]{:S(2)}) collective-permute-start(f32[32,128]{1,0:T(8,128)S(1)} %add.1.refs_0_), channel_id=1, source_target_pairs={{0,4},{1,5},{2,6},{3,7},{4,8},{5,9},{6,10},{7,11},{8,12},{9,13},{1... | collective-permute-start | bytes 49160 | tf_op jit(solution)/shard_map/ppermute | solution.py:303
  127.4 1.2 halves.1
  128.5 0.0 collective-permute-done.5.refs_3_
  128.6 0.0 collective-permute-done.4.refs_2_
  128.6 1.1 collective-permute-done.3.refs_1_
  129.7 4.5 %modes.1 = (f32[4,3,2,8192]{3,2,1,0:T(2,128)}, f32[4,3]{1,0:T(4,128)}) custom-call(f32[32,128]{1,0:T(8,128)S(1)} %add.1.refs_0_, f32[32,128]{1,0:T(8,128)S(1)} %collective-permute-done.3.refs_1_, f32[32,128]{1,0:T(8,128)S(1)} %collective-permute-done.4.refs_2_, f32[32,128]{1,0:T(8,128)S(1)} %collective-permute-done.5.refs_3_, ...), custom_call_target="tpu_custom_call" | custom-call | tf_op jit(solution)/shard_map/modes/pallas_call | solution.py:364
  (1 shorter events, 0.0 us)
Async XLA Ops:
  111.8 5.6 %collective-permute-start.2 = (f32[32,128]{1,0:T(8,128)S(1)}, f32[32,128]{1,0:T(8,128)S(1)}, u32[]{:S(2)}, u32[]{:S(2)}) collective-permute-start(f32[32,128]{1,0:T(8,128)S(1)} %gram.1.refs_0_), channel_id=1, source_target_pairs={{0,3},{1,2},{2,1},{3,0},{4,7},{5,6},{6,5},{7,4},{8,11},{9,10},{10,... | collective-permute-start | bytes 49160 | tf_op jit(solution)/shard_map/ppermute | solution.py:303
  116.0 2.6 %collective-permute-start.1 = (f32[32,128]{1,0:T(8,128)S(1)}, f32[32,128]{1,0:T(8,128)S(1)}, u32[]{:S(2)}, u32[]{:S(2)}) collective-permute-start(f32[32,128]{1,0:T(8,128)S(1)} %gram.1.refs_0_), channel_id=1, source_target_pairs={{0,2},{1,3},{2,0},{3,1},{4,6},{5,7},{6,4},{7,5},{8,10},{9,11},{10,... | collective-permute-start | bytes 49160 | tf_op jit(solution)/shard_map/ppermute | solution.py:303
  116.0 2.6 %collective-permute-start = (f32[32,128]{1,0:T(8,128)S(1)}, f32[32,128]{1,0:T(8,128)S(1)}, u32[]{:S(2)}, u32[]{:S(2)}) collective-permute-start(f32[32,128]{1,0:T(8,128)S(1)} %gram.1.refs_0_), channel_id=1, source_target_pairs={{0,1},{1,0},{2,3},{3,2},{4,5},{5,4},{6,7},{7,6},{8,9},{9,8},{10,11... | collective-permute-start | bytes 49160 | tf_op jit(solution)/shard_map/ppermute | solution.py:303
  118.6 10.0 %collective-permute-start.5 = (f32[32,128]{1,0:T(8,128)S(1)}, f32[32,128]{1,0:T(8,128)S(1)}, u32[]{:S(2)}, u32[]{:S(2)}) collective-permute-start(f32[32,128]{1,0:T(8,128)S(1)} %add.1.refs_0_), channel_id=1, source_target_pairs={{0,8},{1,9},{2,10},{3,11},{4,12},{5,13},{6,14},{7,15},{8,0},{9,1},... | collective-permute-start | bytes 49160 | tf_op jit(solution)/shard_map/ppermute | solution.py:303
  125.0 3.6 %collective-permute-start.4 = (f32[32,128]{1,0:T(8,128)S(1)}, f32[32,128]{1,0:T(8,128)S(1)}, u32[]{:S(2)}, u32[]{:S(2)}) collective-permute-start(f32[32,128]{1,0:T(8,128)S(1)} %add.1.refs_0_), channel_id=1, source_target_pairs={{0,12},{1,13},{2,14},{3,15},{4,0},{5,1},{6,2},{7,3},{8,4},{9,5},{1... | collective-permute-start | bytes 49160 | tf_op jit(solution)/shard_map/ppermute | solution.py:303
  125.0 4.7 %collective-permute-start.3 = (f32[32,128]{1,0:T(8,128)S(1)}, f32[32,128]{1,0:T(8,128)S(1)}, u32[]{:S(2)}, u32[]{:S(2)}) collective-permute-start(f32[32,128]{1,0:T(8,128)S(1)} %add.1.refs_0_), channel_id=1, source_target_pairs={{0,4},{1,5},{2,6},{3,7},{4,8},{5,9},{6,10},{7,11},{8,12},{9,13},{1... | collective-permute-start | bytes 49160 | tf_op jit(solution)/shard_map/ppermute | solution.py:303

commit v6 on v5

--- a/solution.py
+++ b/solution.py
@@ -102,7 +102,7 @@
 
 
 def transform_kernel(
-    owners, table_hbm, x_hbm, start_hbm, out_ref, first_ref, table_ref, x_ref, start_ref, in_sem, small_sem
+    owners, table_hbm, x_hbm, start_hbm, out_ref, start_ref, table_ref, x_ref, in_sem, small_sem
 ):
     times, points = x_hbm.shape
     local_blocks = times // NFFT
@@ -119,7 +119,6 @@
     start_copy.start()
     for i in range(len(chunks)):
         fetch(i).start()
-    bins = FREQS // owners
     table_copy.wait()
     high, middle, low = split3(table_ref[...])
     wide = jnp.concatenate([high, middle, low, high, middle, high], axis=1)
@@ -131,10 +130,7 @@
         for block in range(BLOCKS):
             rows, cols = slice(block * 8, block * 8 + 8), slice(block * size, block * size + size)
             out_ref[:, rows, at : at + size] = out[:, cols].reshape(owners, 8, size)
-        if i == 1:
-            start_copy.wait()
-            first = lax.axis_index("tm") * bins
-            first_ref[...] = first_vectors(start_ref[...], first, bins)
+    start_copy.wait()
 
 
 def transform(snapshots, start, owners):
@@ -148,12 +144,11 @@
         out_specs=[VMEM, VMEM],
         out_shape=[
             pltpu.VMEM(shape, F32),
-            jax.ShapeDtypeStruct((16, NB * FREQS // owners), F32),
+            pltpu.VMEM(start.shape, F32),
         ],
         scratch_shapes=[
             pltpu.VMEM((2 * FREQS, NFFT), F32),
             pltpu.VMEM(snapshots.shape, F32),
-            pltpu.VMEM(start.shape, F32),
             pltpu.SemaphoreType.DMA((count,)),
             pltpu.SemaphoreType.DMA((2,)),
         ],
@@ -162,13 +157,16 @@
     )(table, snapshots, start)
 
 
-def gram_kernel(scale, s_ref, out_ref):
+def gram_kernel(scale, s_ref, start_ref, out_ref, first_ref):
     points = s_ref.shape[2]
     rows, half = 2 * NB * BINS, NB * BINS
     sums = jnp.zeros((2 * rows, rows), F32)
     for at, size in column_chunks(points):
         high, low = split(s_ref[:, :, at : at + size].reshape(rows, size))
         sums += dot_rows(jnp.concatenate([high, low], axis=0), high)
+        if at == 0:
+            first = lax.axis_index("tm") * BINS
+            first_ref[...] = first_vectors(start_ref[...], first, BINS)
     cross = sums[rows:]
     full = (sums[:rows] + (cross + cross.T)) * scale
     row, col = iota((rows, rows), 0), iota((rows, rows), 1)
@@ -186,15 +184,15 @@
     out_ref[...] = packed
 
 
-def partial_gram(spectra, total_points):
+def partial_gram(spectra, start, total_points):
     return pl.pallas_call(
         functools.partial(gram_kernel, 1.0 / (NB * total_points)),
-        in_specs=[VMEM],
-        out_specs=VMEM,
-        out_shape=pltpu.VMEM((NB, NB * BINS), F32),
+        in_specs=[VMEM, VMEM],
+        out_specs=[VMEM, VMEM],
+        out_shape=[pltpu.VMEM((NB, NB * BINS), F32), pltpu.VMEM((16, NB * BINS), F32)],
         compiler_params=pltpu.CompilerParams(vmem_limit_bytes=VMEM_LIMIT),
         name="gram",
-    )(spectra)
+    )(spectra, start)
 
 
 def bin_ones(lanes, bins):
@@ -352,7 +350,10 @@
         halves_kernel,
         in_specs=[VMEM],
         out_specs=[VMEM, VMEM],
-        out_shape=[pltpu.VMEM(shape, BF16), pltpu.VMEM(shape, BF16)],
+        out_shape=[
+            pltpu.VMEM(shape, BF16),
+            pltpu.VMEM(shape, BF16),
+        ],
         compiler_params=pltpu.CompilerParams(vmem_limit_bytes=8 * 1024 * 1024),
         cost_estimate=pl.CostEstimate(flops=10**7, bytes_accessed=10**6, transcendentals=0),
         name="halves",
@@ -381,10 +382,10 @@
     bins = FREQS // tm_count
     snapshots = pltpu.with_memory_space_constraint(snapshots, pltpu.HBM)
     start = pltpu.with_memory_space_constraint(start.transpose(1, 2, 3, 0), pltpu.HBM)
-    sent, own = transform(snapshots, start, tm_count)
+    sent, kept = transform(snapshots, start, tm_count)
     spectra = lax.all_to_all(sent, "tm", split_axis=0, concat_axis=0, tiled=True)
     spectra = pltpu.with_memory_space_constraint(spectra, pltpu.VMEM)
-    gram = partial_gram(spectra, total_points)
+    gram, own = partial_gram(spectra, kept, total_points)
     near = add(exchange(gram, [lambda i, n, k=k: i ^ k for k in (1, 2, 3)]))
     grams = exchange(near, [lambda i, n, k=k: (i + 4 * k) % n for k in (1, 3, 2)])
     modes, energies = modes_of(grams, own, *halves_of(spectra), bins)

time: 134 us -> 134 us (level)
  no operation moved by 1% of the time
where the time goes in v6:
time: 134 us
  blocking collectives  102 us (76%)
  Pallas kernels  14.4 us (11%)
  starting transfers between devices  13.5 us (10%)
  waiting for transfers between devices  3.24 us (2%)
    all_to_all x1, blocking collectives, on_device(): lax.all_to_all(sent, 'tm', split_axis=0, concat_axis=0, tiled=True)  102 us
    ppermute x6, starting transfers between devices, exchange(): parts.append(lax.ppermute(part, 'space', pairs))  13.5 us
    pallas_call x1, Pallas kernels, transform(): pl.pallas_call(functools.partial(transform_kernel, owners), in_specs=[HBM...  5.45 us
    pallas_call x1, Pallas kernels, modes_of(): pl.pallas_call(functools.partial(modes_kernel, bins), in_specs=[VMEM] * (...  4.47 us
    pallas_call x1, Pallas kernels, partial_gram(): pl.pallas_call(functools.partial(gram_kernel, 1.0 / (NB * total_points)),...  3.26 us
    ppermute x6, waiting for transfers between devices, exchange(): parts.append(lax.ppermute(part, 'space', pairs))  3.24 us
  transfers between devices with their start and end apart: 6, of which 3 were waited for; matrix products, arithmetic and copies ran while one was open for 0% of the time, Pallas kernels for 1%

profile of v6, /device:TPU:1, one launch (start us, length us, event | category | flops | bytes accessed | tf_op | source)
XLA Modules:
  0.0 133.9 jit_solution(17665826835743962846)
XLA Ops:
  0.6 5.5 %transform.1 = (f32[16,16,8192]{2,1,0:T(8,128)S(1)}, f32[2,3,32,64]{3,2,1,0:T(8,128)S(1)}) custom-call(f32[128,128]{1,0:T(8,128)} %constant.2.clone.table_hbm, f32[256,8192]{1,0:T(8,128)} %x_hbm.1, f32[2,3,32,64]{3,2,1,0:T(8,128)} %bitcast.2), custom_call_target="tpu_custom_call" | custom-call | tf_op jit(solution)/shard_map/transform/pallas_call | solution.py:141
  6.1 102.1 %all_to_all.5.s_ref = f32[16,16,8192]{2,1,0:T(8,128)S(1)} all-to-all(f32[16,16,8192]{2,1,0:T(8,128)S(1)} %get-tuple-element.10), channel_id=1, replica_groups=mesh['tm'=16,'space'=16] {'tm'}, dimensions={0} | all-to-all | bytes 16777216 | tf_op jit(solution)/shard_map/all_to_all | solution.py:386
  108.2 3.3 %gram.1 = (f32[32,128]{1,0:T(8,128)S(1)}, f32[16,128]{1,0:T(8,128)S(1)}) custom-call(f32[16,16,8192]{2,1,0:T(8,128)S(1)} %all_to_all.5.s_ref, f32[2,3,32,64]{3,2,1,0:T(8,128)S(1)} %get-tuple-element.11.start_ref), custom_call_target="tpu_custom_call" | custom-call | tf_op jit(solution)/shard_map/gram/pallas_call | solution.py:188
  111.5 4.2 %collective-permute-start.2 = (f32[32,128]{1,0:T(8,128)S(1)}, f32[32,128]{1,0:T(8,128)S(1)}, u32[]{:S(2)}, u32[]{:S(2)}) collective-permute-start(f32[32,128]{1,0:T(8,128)S(1)} %get-tuple-element.12.refs_0_), channel_id=1, source_target_pairs={{0,3},{1,2},{2,1},{3,0},{4,7},{5,6},{6,5},{7,4},{8,11},{9,10},{10,... | collective-permute-start | bytes 49160 | tf_op jit(solution)/shard_map/ppermute | solution.py:301
  115.6 0.0 collective-permute-start.1
  115.6 0.5 collective-permute-start
  116.1 0.9 collective-permute-done.2.refs_3_
  117.1 1.2 collective-permute-done.1.refs_2_
  118.2 0.0 collective-permute-done.refs_1_
  118.2 6.4 %collective-permute-start.5 = (f32[32,128]{1,0:T(8,128)S(1)}, f32[32,128]{1,0:T(8,128)S(1)}, u32[]{:S(2)}, u32[]{:S(2)}) collective-permute-start(f32[32,128]{1,0:T(8,128)S(1)} %add.1.refs_0_), channel_id=1, source_target_pairs={{0,8},{1,9},{2,10},{3,11},{4,12},{5,13},{6,14},{7,15},{8,0},{9,1},... | collective-permute-start | bytes 49160 | tf_op jit(solution)/shard_map/ppermute | solution.py:301
  124.7 0.0 collective-permute-start.4
  124.7 2.4 %collective-permute-start.3 = (f32[32,128]{1,0:T(8,128)S(1)}, f32[32,128]{1,0:T(8,128)S(1)}, u32[]{:S(2)}, u32[]{:S(2)}) collective-permute-start(f32[32,128]{1,0:T(8,128)S(1)} %add.1.refs_0_), channel_id=1, source_target_pairs={{0,4},{1,5},{2,6},{3,7},{4,8},{5,9},{6,10},{7,11},{8,12},{9,13},{1... | collective-permute-start | bytes 49160 | tf_op jit(solution)/shard_map/ppermute | solution.py:301
  127.0 1.2 halves.1
  128.2 0.0 collective-permute-done.5.refs_3_
  128.2 0.0 collective-permute-done.4.refs_2_
  128.2 1.1 collective-permute-done.3.refs_1_
  129.4 4.5 %modes.1 = (f32[4,3,2,8192]{3,2,1,0:T(2,128)}, f32[4,3]{1,0:T(4,128)}) custom-call(f32[32,128]{1,0:T(8,128)S(1)} %add.1.refs_0_, f32[32,128]{1,0:T(8,128)S(1)} %collective-permute-done.3.refs_1_, f32[32,128]{1,0:T(8,128)S(1)} %collective-permute-done.4.refs_2_, f32[32,128]{1,0:T(8,128)S(1)} %collective-permute-done.5.refs_3_, ...), custom_call_target="tpu_custom_call" | custom-call | tf_op jit(solution)/shard_map/modes/pallas_call | solution.py:365
  (1 shorter events, 0.0 us)
Async XLA Ops:
  111.5 5.6 %collective-permute-start.2 = (f32[32,128]{1,0:T(8,128)S(1)}, f32[32,128]{1,0:T(8,128)S(1)}, u32[]{:S(2)}, u32[]{:S(2)}) collective-permute-start(f32[32,128]{1,0:T(8,128)S(1)} %get-tuple-element.12.refs_0_), channel_id=1, source_target_pairs={{0,3},{1,2},{2,1},{3,0},{4,7},{5,6},{6,5},{7,4},{8,11},{9,10},{10,... | collective-permute-start | bytes 49160 | tf_op jit(solution)/shard_map/ppermute | solution.py:301
  115.6 2.6 %collective-permute-start.1 = (f32[32,128]{1,0:T(8,128)S(1)}, f32[32,128]{1,0:T(8,128)S(1)}, u32[]{:S(2)}, u32[]{:S(2)}) collective-permute-start(f32[32,128]{1,0:T(8,128)S(1)} %get-tuple-element.12.refs_0_), channel_id=1, source_target_pairs={{0,2},{1,3},{2,0},{3,1},{4,6},{5,7},{6,4},{7,5},{8,10},{9,11},{10,... | collective-permute-start | bytes 49160 | tf_op jit(solution)/shard_map/ppermute | solution.py:301
  115.6 2.6 %collective-permute-start = (f32[32,128]{1,0:T(8,128)S(1)}, f32[32,128]{1,0:T(8,128)S(1)}, u32[]{:S(2)}, u32[]{:S(2)}) collective-permute-start(f32[32,128]{1,0:T(8,128)S(1)} %get-tuple-element.12.refs_0_), channel_id=1, source_target_pairs={{0,1},{1,0},{2,3},{3,2},{4,5},{5,4},{6,7},{7,6},{8,9},{9,8},{10,11... | collective-permute-start | bytes 49160 | tf_op jit(solution)/shard_map/ppermute | solution.py:301
  118.2 10.0 %collective-permute-start.5 = (f32[32,128]{1,0:T(8,128)S(1)}, f32[32,128]{1,0:T(8,128)S(1)}, u32[]{:S(2)}, u32[]{:S(2)}) collective-permute-start(f32[32,128]{1,0:T(8,128)S(1)} %add.1.refs_0_), channel_id=1, source_target_pairs={{0,8},{1,9},{2,10},{3,11},{4,12},{5,13},{6,14},{7,15},{8,0},{9,1},... | collective-permute-start | bytes 49160 | tf_op jit(solution)/shard_map/ppermute | solution.py:301
  124.7 3.6 %collective-permute-start.4 = (f32[32,128]{1,0:T(8,128)S(1)}, f32[32,128]{1,0:T(8,128)S(1)}, u32[]{:S(2)}, u32[]{:S(2)}) collective-permute-start(f32[32,128]{1,0:T(8,128)S(1)} %add.1.refs_0_), channel_id=1, source_target_pairs={{0,12},{1,13},{2,14},{3,15},{4,0},{5,1},{6,2},{7,3},{8,4},{9,5},{1... | collective-permute-start | bytes 49160 | tf_op jit(solution)/shard_map/ppermute | solution.py:301
  124.7 4.7 %collective-permute-start.3 = (f32[32,128]{1,0:T(8,128)S(1)}, f32[32,128]{1,0:T(8,128)S(1)}, u32[]{:S(2)}, u32[]{:S(2)}) collective-permute-start(f32[32,128]{1,0:T(8,128)S(1)} %add.1.refs_0_), channel_id=1, source_target_pairs={{0,4},{1,5},{2,6},{3,7},{4,8},{5,9},{6,10},{7,11},{8,12},{9,13},{1... | collective-permute-start | bytes 49160 | tf_op jit(solution)/shard_map/ppermute | solution.py:301
